TPU v7x, 128 devices: a whole 4x4x4 slice. The times are simulated.
128 devices in a mesh: row: 8 (over z_lo, y), col: 16 (over x, z_hi, core).
Axes of the slice: x: 4, y: 4, z: 4 (z_hi: 2, z_lo: 2; z = z_hi * 2 + z_lo), core: 2. Of those that a mesh axis runs over, the one named last changes fastest.
Arguments:
- children: float32 [24576, 12288], P('row', 'col'), as said below
- parent: float32 [16384, 16384], P('row', 'col'), as said below
- relay_map: int32 [2, 46], replicated, may hold values from 0 to 63, as said below
Outputs:
- parent_out: float32 [16384, 16384], P('row', 'col')
- child_factor: float32 [24576, 512], P('row', 'col')
Inputs may be any that keep to these rules, and one draw needn't show every extreme that they name: children holds two symmetric positive definite fronts. parent is symmetric positive definite. relay_map[k, j - 2] is the parent block that receives child k's block j (blocks of 256); it lies in [8 * (j // 6), 8 * (j // 6) + 8); entries of one child are distinct.
All inputs are finite; a program needn't handle non-finite values.
Results may differ from a plain program's by a relative error of at most 0.0001.
Values sent between devices are 32-bit elements; how exact they have to be, the bound alone decides.
A program may use at most 192 MiB of HBM per device.

v0:
```python
import jax
import jax.numpy as jnp
from jax import lax
from jax.sharding import PartitionSpec as P

NB = 256
PIV_C = 512
PIV_P = 512


highest = lax.Precision.HIGHEST


def spread(block, axis, owner):
    block = jnp.where(lax.axis_index(axis) == owner, block, jnp.zeros_like(block))
    return lax.psum(block, axis)


def from_behind(block, axis, distance):
    devices = range(lax.axis_size(axis))
    route = [(i - distance, i) for i in devices if i - distance in devices]
    return lax.ppermute(block, axis, route)


def partner(block, axis, distance):
    count = lax.axis_size(axis)
    route = []
    for low in range(count):
        high = low | 1 << distance
        if high != low and high < count:
            route += [(low, high), (high, low)]
    return lax.ppermute(block, axis, route)


def lower_solve(diag_factor, right_side):
    return lax.linalg.triangular_solve(diag_factor, right_side, left_side=True, lower=True)


def lookup(lookup_table, wanted):
    positions = jnp.arange(lookup_table.shape[0], dtype=jnp.int32)
    return jnp.sum(
        jnp.where(positions[None, :] == wanted[:, None], lookup_table[None, :], 0), axis=1
    )


def block_slots(lookup_table, blocks, group_size, group_span):
    usable = blocks >= PIV_C // NB
    targets = lookup(lookup_table, blocks - PIV_C // NB)
    return (targets - blocks // group_size * group_span, usable)


def spread_columns(blocks_view, targets, usable, width_blocks):
    places = jnp.arange(width_blocks, dtype=jnp.int32)
    selector = jnp.where(
        usable[:, None] & ((targets % width_blocks)[:, None] == places[None, :]), 1.0, 0.0
    ).astype(jnp.float32)
    return jnp.einsum("rub,uq->rqb", blocks_view, selector, precision=highest)


def spread_rows(blocks_view, targets, usable, height_blocks):
    places = jnp.arange(height_blocks, dtype=jnp.int32)
    selector = jnp.where(usable[:, None] & (targets[:, None] == places[None, :]), 1.0, 0.0).astype(
        jnp.float32
    )
    return jnp.einsum("tbx,tp->pbx", blocks_view, selector, precision=highest)


def eliminate(matrix, row_ids, col_ids, pivots, move_panel, move_rows):
    height, breadth = matrix.shape
    pieces = []
    for panel_index in range(pivots // NB):
        low_edge = panel_index * NB
        high_edge = low_edge + NB
        panel_cols = move_panel(matrix[:, low_edge:high_edge])
        offset = jnp.clip(low_edge - row_ids[0], 0, height - NB)
        own_rows = lax.dynamic_slice_in_dim(matrix, offset, NB, 0)
        own_diag = lax.dynamic_slice_in_dim(panel_cols, offset, NB, 0)
        joined = move_rows(jnp.concatenate([own_rows, own_diag], axis=1))
        pivot_rows = joined[:, :breadth]
        diag_factor = jnp.linalg.cholesky(joined[:, breadth:])
        beneath = row_ids >= high_edge
        row_part = jnp.where(beneath[:, None], lower_solve(diag_factor, panel_cols.T).T, 0.0)
        col_part = jnp.where(
            (col_ids >= high_edge)[:, None], lower_solve(diag_factor, pivot_rows).T, 0.0
        )
        matrix = matrix - jnp.dot(row_part, col_part.T, precision=highest)
        placed = lax.dynamic_update_slice_in_dim(
            jnp.zeros((height, NB), jnp.float32), diag_factor, offset, 0
        )
        inside = (row_ids >= low_edge) & (row_ids < high_edge)
        pieces.append(
            jnp.where(beneath[:, None], row_part, jnp.where(inside[:, None], placed, 0.0))
        )
    return (matrix, jnp.concatenate(pieces, axis=1))


def local(children, parent, relay_map):
    row_index = lax.axis_index("row")
    col_index = lax.axis_index("col")
    parity = row_index % 2
    child_level = row_index // 2
    child_height, child_width = children.shape
    parent_height, parent_width = parent.shape
    child_row_ids = child_level * child_height + jnp.arange(child_height, dtype=jnp.int32)
    child_col_ids = col_index * child_width + jnp.arange(child_width, dtype=jnp.int32)

    def child_panel_move(piece):
        return spread(piece, "col", 0)

    def spread_pivot_rows(joined):
        levels = (lax.axis_size("row") // 2).bit_length() - 1
        for section in range(levels):
            arrived = from_behind(joined, "row", 2 << section)
            chosen = (child_level >= 1 << section) & (child_level < 2 << section)
            joined = jnp.where(chosen, arrived, joined)
        return joined

    reduced, factor = eliminate(
        children, child_row_ids, child_col_ids, PIV_C, child_panel_move, spread_pivot_rows
    )
    share = PIV_C // lax.axis_size("col")
    child_factor = lax.dynamic_slice_in_dim(factor, col_index * share, share, 1)
    keep_mask = (child_row_ids >= PIV_C)[:, None] & (child_col_ids >= PIV_C)[None, :]
    remainder = jnp.where(keep_mask, reduced, 0.0)
    col_blocks = child_width // NB
    group_size = 2 * col_blocks
    parent_col_blocks = parent_width // NB
    group_span = 2 * parent_col_blocks
    half_height = child_height // 2
    own_map = jnp.where(parity == 0, relay_map[0], relay_map[1])
    other_map = jnp.where(parity == 0, relay_map[1], relay_map[0])
    partner_col = col_index + 1 - 2 * (col_index % 2)
    own_col_blocks = col_index * col_blocks + jnp.arange(col_blocks, dtype=jnp.int32)
    partner_col_blocks = partner_col * col_blocks + jnp.arange(col_blocks, dtype=jnp.int32)
    row_blocks = (
        child_level * 2 * group_size + parity * group_size + jnp.arange(group_size, dtype=jnp.int32)
    )
    own_row_slots, own_row_usable = block_slots(own_map, row_blocks, group_size, group_span)
    other_row_slots, other_row_usable = block_slots(other_map, row_blocks, group_size, group_span)
    blocks_view = remainder.reshape(child_height, col_blocks, NB)
    targets, usable = block_slots(own_map, own_col_blocks, group_size, group_span)
    leaving = usable & (targets // parent_col_blocks != col_index % 2)
    kept = spread_columns(
        blocks_view, targets, usable & jnp.logical_not(leaving), parent_col_blocks
    )
    outgoing = jnp.where(leaving[None, :, None], blocks_view, 0.0).reshape(
        child_height, child_width
    )
    incoming = partner(outgoing, "col", 0).reshape(child_height, col_blocks, NB)
    partner_targets, partner_usable = block_slots(
        own_map, partner_col_blocks, group_size, group_span
    )
    partner_leaving = partner_usable & (partner_targets // parent_col_blocks != partner_col % 2)
    arrived = spread_columns(incoming, partner_targets, partner_leaving, parent_col_blocks)
    widened = (kept + arrived).reshape(2, half_height, parent_width)
    staying = lax.dynamic_index_in_dim(widened, parity, 0, keepdims=False)
    going = lax.dynamic_index_in_dim(widened, 1 - parity, 0, keepdims=False)
    received = partner(going, "row", 0)
    contribution = spread_rows(
        staying.reshape(group_size, NB, parent_width), own_row_slots, own_row_usable, group_span
    )
    contribution = contribution + spread_rows(
        received.reshape(group_size, NB, parent_width),
        other_row_slots,
        other_row_usable,
        group_span,
    )
    combined = parent + contribution.reshape(parent_height, parent_width)
    parent_row_ids = row_index * parent_height + jnp.arange(parent_height, dtype=jnp.int32)
    parent_col_ids = col_index * parent_width + jnp.arange(parent_width, dtype=jnp.int32)

    def parent_panel_move(piece):
        return spread(piece, "col", 0)

    def parent_rows_move(joined):
        return spread(joined, "row", 0)

    reduced_parent, parent_factor = eliminate(
        combined, parent_row_ids, parent_col_ids, PIV_P, parent_panel_move, parent_rows_move
    )
    padded = jnp.concatenate(
        [parent_factor, jnp.zeros((parent_height, parent_width - PIV_P), jnp.float32)], axis=1
    )
    pivot_cols = parent_col_ids < PIV_P
    pivot_rows = parent_row_ids < PIV_P
    parent_out = jnp.where(
        pivot_cols[None, :], padded, jnp.where(pivot_rows[:, None], 0.0, reduced_parent)
    )
    return (parent_out, child_factor)


def solution(mesh):
    return jax.shard_map(
        local,
        mesh=mesh,
        in_specs=(P("row", "col"), P("row", "col"), P()),
        out_specs=(P("row", "col"), P("row", "col")),
        check_vma=False,
    )
```

profile of v0, /device:TPU:57, one launch (start us, length us, event | category | flops | bytes accessed | tf_op | source)
XLA Modules:
  0.0 1553.8 jit_solution(1680605014874526064)
XLA Ops:
  23.6 145.5 %all-reduce.8.cloned.1.call-done = f32[3072,256]{0,1:T(8,128)} async-done(((f32[3072,256]{0,1:T(8,128)}), f32[3072,256]{0,1:T(8,128)}) %all-reduce.8.cloned.1.call-update) | async-done | bytes 3145744 | tf_op jit(solution)/shard_map/psum | solution.py:16
  171.6 25.3 %collective-permute-done = f32[256,1024]{0,1:T(8,128)S(1)} collective-permute-done((f32[256,1024]{0,1:T(8,128)S(1)}, f32[256,1024]{0,1:T(8,128)S(1)}, u32[]{:S(2)}, u32[]{:S(2)}) %collective-permute-start) | collective-permute-done | bytes 1048608 | tf_op jit(solution)/shard_map/ppermute | solution.py:22
  199.2 22.1 %collective-permute-done.1 = f32[256,1024]{0,1:T(8,128)S(1)} collective-permute-done((f32[256,1024]{0,1:T(8,128)S(1)}, f32[256,1024]{0,1:T(8,128)S(1)}, u32[]{:S(2)}, u32[]{:S(2)}) %collective-permute-start.1) | collective-permute-done | bytes 1048608 | tf_op jit(solution)/shard_map/ppermute | solution.py:22
  221.6 11.7 cholesky.214
  243.9 11.7 cholesky.231
  262.8 19.7 %custom-call.28 = f32[2,128,128]{1,2,0:T(8,128)S(1)} custom-call(f32[2,128,128]{2,1,0:T(8,128)S(1)} %get-tuple-element.63), custom_call_target="InvertDiagBlocksLowerTriangular" | custom-call | tf_op jit(solution)/shard_map/triangular_solve/custom-call.0 | solution.py:36
  290.3 11.8 convolution_subtract_fusion
  309.2 144.9 %all-reduce.10.cloned.1.call-done = f32[3072,256]{0,1:T(8,128)} async-done(((f32[3072,256]{0,1:T(8,128)}), f32[3072,256]{0,1:T(8,128)}) %all-reduce.10.cloned.1.call-update) | async-done | bytes 3145744 | tf_op jit(solution)/shard_map/psum | solution.py:16
  456.6 25.3 %collective-permute-done.2 = f32[256,1024]{0,1:T(8,128)S(1)} collective-permute-done((f32[256,1024]{0,1:T(8,128)S(1)}, f32[256,1024]{0,1:T(8,128)S(1)}, u32[]{:S(2)}, u32[]{:S(2)}) %collective-permute-start.2) | collective-permute-done | bytes 1048608 | tf_op jit(solution)/shard_map/ppermute | solution.py:22
  487.1 20.4 %collective-permute-done.3 = f32[256,1024]{0,1:T(8,128)} collective-permute-done((f32[256,1024]{0,1:T(8,128)}, f32[256,1024]{0,1:T(8,128)}, u32[]{:S(2)}, u32[]{:S(2)}) %collective-permute-start.3) | collective-permute-done | bytes 1048608 | tf_op jit(solution)/shard_map/ppermute | solution.py:22
  509.1 11.7 cholesky.248
  531.4 11.7 cholesky.265
  551.6 19.7 %custom-call.31 = f32[2,128,128]{1,2,0:T(8,128)S(1)} custom-call(f32[2,128,128]{2,1,0:T(8,128)S(1)} %get-tuple-element.65), custom_call_target="InvertDiagBlocksLowerTriangular" | custom-call | tf_op jit(solution)/shard_map/triangular_solve/custom-call.0 | solution.py:36
  580.3 15.9 %broadcast_select_fusion = (f32[3072,768]{0,1:T(8,128)}, f32[3072,768]{0,1:T(8,128)}) fusion(pred[768]{0:T(1024)(128)(4,1)S(1)} %broadcast_in_dim.282, f32[3072,768]{0,1:T(8,128)} %copy-done.1, f32[128,768]{1,0:T(8,128)S(1)} %fusion.40, f32[128,768]{1,0:T(8,128)S(1)} %fusion.41, pred[768]{0:T(1024)(128)(4,1)S(1)} %copy-done.29, ...), kind=kOutput, calls=%fused_computation.19 | convolution fusion | flops 7259160576 | bytes 32248320 | tf_op jit(solution)/shard_map/dot_general | solution.py:86
  599.9 13.3 copy.80
  613.2 26.8 %fusion.120 = f32[4,3072,256]{2,0,1:T(4,128)} fusion(f32[3072,3,256]{2,1,0:T(4,128)} %copy.80, s32[3]{0:T(128)S(1)} %get-tuple-element.257, pred[3]{0:T(512)(128)(4,1)S(1)} %copy-done.24), kind=kOutput, calls=%fused_computation.225 | convolution fusion | flops 113246240 | bytes 22020112 | tf_op jit(solution)/shard_map/rub,uq->rqb/dot_general | solution.py:57
  640.0 13.3 copy.81
  653.3 29.2 %add_bitcast_fusion = f32[3072,4,256]{2,1,0:T(4,128)} fusion(f32[4,3072,256]{2,0,1:T(4,128)} %fusion.120, f32[3072,3,256]{2,1,0:T(4,128)} %copy.81, s32[3]{0:T(128)S(1)} %get-tuple-element.256, pred[3]{0:T(512)(128)(4,1)S(1)} %get-tuple-element.213), kind=kOutput, calls=%fused_computation.8 | convolution fusion | flops 116391968 | bytes 34603024 | tf_op jit(solution)/shard_map/rub,uq->rqb/dot_general | solution.py:57
  682.5 15.7 %reshape.347 = f32[2,1536,1024]{2,1,0:T(8,128)} reshape(f32[3072,4,256]{2,1,0:T(4,128)} %add_bitcast_fusion) | data formatting | bytes 25165824 | tf_op jit(solution)/shard_map/reshape | solution.py:155
  698.2 11.9 dynamic-slice_bitcast_fusion
  720.2 15.7 %fusion.2 = f32[8,256,1024]{2,0,1:T(8,128)S(1)} fusion(f32[6,256,1024]{2,1,0:T(8,128)} %bitcast.205, s32[6]{0:T(128)S(1)} %get-tuple-element.259, pred[6]{0:T(512)(128)(4,1)S(1)} %fusion.150), kind=kOutput, calls=%fused_computation.13 | convolution fusion | flops 150995088 | bytes 14680094 | tf_op jit(solution)/shard_map/tbx,tp->pbx/dot_general | solution.py:65
  735.8 111.6 %collective-permute-done.5 = f32[1536,1024]{1,0:T(8,128)} collective-permute-done((f32[1536,1024]{1,0:T(8,128)}, f32[1536,1024]{1,0:T(8,128)}, u32[]{:S(2)}, u32[]{:S(2)}) %collective-permute-start.5) | collective-permute-done | bytes 6291488 | tf_op jit(solution)/shard_map/ppermute | solution.py:32
  847.5 16.6 %fusion.4 = f32[8,256,1024]{2,0,1:T(8,128)} fusion(f32[8,256,1024]{2,0,1:T(8,128)S(1)} %fusion.2, f32[6,256,1024]{2,1,0:T(8,128)} %bitcast.29, s32[6]{0:T(128)S(1)} %get-tuple-element.258, pred[6]{0:T(512)(128)(4,1)S(1)} %fusion.150), kind=kOutput, calls=%fused_computation.23 | convolution fusion | flops 153092240 | bytes 23068702 | tf_op jit(solution)/shard_map/tbx,tp->pbx/dot_general | solution.py:65
  884.6 11.9 add.332
  903.7 136.6 %all-reduce.12.cloned.1.call-done = f32[2048,256]{0,1:T(8,128)} async-done(((f32[2048,256]{0,1:T(8,128)}), f32[2048,256]{0,1:T(8,128)}) %all-reduce.12.cloned.1.call-update) | async-done | bytes 2097168 | tf_op jit(solution)/shard_map/psum | solution.py:16
  1046.0 72.3 %all-reduce.14.cloned.1.call-done = f32[256,1280]{0,1:T(8,128)} async-done(((f32[256,1280]{0,1:T(8,128)}), f32[256,1280]{0,1:T(8,128)}) %all-reduce.14.cloned.1.call-update) | async-done | bytes 1310736 | tf_op jit(solution)/shard_map/psum | solution.py:16
  1147.9 11.7 cholesky.299
  1174.4 20.5 %custom-call.34 = f32[2,128,128]{1,2,0:T(8,128)S(1)} custom-call(f32[2,128,128]{2,1,0:T(8,128)} %get-tuple-element.67), custom_call_target="InvertDiagBlocksLowerTriangular" | custom-call | tf_op jit(solution)/shard_map/triangular_solve/custom-call.5 | solution.py:36
  1235.2 131.9 %all-reduce.16.cloned.1.call-done = f32[2048,256]{0,1:T(8,128)} async-done(((f32[2048,256]{0,1:T(8,128)}), f32[2048,256]{0,1:T(8,128)}) %all-reduce.16.cloned.1.call-update) | async-done | bytes 2097168 | tf_op jit(solution)/shard_map/psum | solution.py:16
  1380.9 64.2 %all-reduce.18.cloned.1.call-done = f32[256,1280]{0,1:T(8,128)} async-done(((f32[256,1280]{0,1:T(8,128)}), f32[256,1280]{0,1:T(8,128)}) %all-reduce.18.cloned.1.call-update) | async-done | bytes 1310736 | tf_op jit(solution)/shard_map/psum | solution.py:16
  1488.0 19.9 %custom-call.37 = f32[2,128,128]{1,2,0:T(8,128)S(1)} custom-call(f32[2,128,128]{2,1,0:T(8,128)S(1)} %get-tuple-element.69), custom_call_target="InvertDiagBlocksLowerTriangular" | custom-call | tf_op jit(solution)/shard_map/triangular_solve/custom-call.5 | solution.py:36
  1523.6 13.7 maximum_select_fusion
  (297 shorter events, 315.1 us)
Async XLA Ops:
  7.2 161.9 %all-reduce.8.cloned.1.call-start = ((), (), s32[]{:S(2)}) async-start(), calls=%async_computation | async-start | bytes 6291456 | tf_op jit(solution)/shard_map/psum | solution.py:16
  20.8 433.3 %all-reduce.10.cloned.1.call-start = ((), (), s32[]{:S(2)}) async-start(), calls=%async_computation.1 | async-start | bytes 6291456 | tf_op jit(solution)/shard_map/psum | solution.py:16
  170.3 26.6 %collective-permute-start = (f32[256,1024]{0,1:T(8,128)S(1)}, f32[256,1024]{0,1:T(8,128)S(1)}, u32[]{:S(2)}, u32[]{:S(2)}) collective-permute-start(f32[256,1024]{0,1:T(8,128)S(1)} %pad_maximum_fusion), channel_id=1, source_target_pairs={{0,32},{16,48},{32,64},{48,80},{64,96},{80,112},{1,33},{17,49},{33... | collective-permute-start | bytes 3145736 | tf_op jit(solution)/shard_map/ppermute | solution.py:22
  197.0 24.2 %collective-permute-start.1 = (f32[256,1024]{0,1:T(8,128)S(1)}, f32[256,1024]{0,1:T(8,128)S(1)}, u32[]{:S(2)}, u32[]{:S(2)}) collective-permute-start(f32[256,1024]{0,1:T(8,128)S(1)} %broadcast_select_fusion.2), channel_id=1, source_target_pairs={{0,64},{16,80},{32,96},{48,112},{1,65},{17,81},{33,97},{49,113},{2... | collective-permute-start | bytes 3145736 | tf_op jit(solution)/shard_map/ppermute | solution.py:22
  282.5 4.7 copy-start.12
  290.2 11.8 copy-start.6
  307.6 732.8 %all-reduce.12.cloned.1.call-start = ((), (), s32[]{:S(2)}) async-start(), calls=%async_computation.2 | async-start | bytes 4194304 | tf_op jit(solution)/shard_map/psum | solution.py:16
  309.2 175.4 %copy-start.31 = (s32[2,46]{1,0:T(2,128)S(1)}, s32[2,46]{1,0:T(2,128)}, u32[]{:S(2)}) copy-start(s32[2,46]{1,0:T(2,128)} %param.14) | copy-start | bytes 1108
  455.3 26.6 %collective-permute-start.2 = (f32[256,1024]{0,1:T(8,128)S(1)}, f32[256,1024]{0,1:T(8,128)S(1)}, u32[]{:S(2)}, u32[]{:S(2)}) collective-permute-start(f32[256,1024]{0,1:T(8,128)S(1)} %pad_maximum_fusion.1), channel_id=1, source_target_pairs={{0,32},{16,48},{32,64},{48,80},{64,96},{80,112},{1,33},{17,49},{33... | collective-permute-start | bytes 3145736 | tf_op jit(solution)/shard_map/ppermute | solution.py:22
  483.0 24.5 %collective-permute-start.3 = (f32[256,1024]{0,1:T(8,128)}, f32[256,1024]{0,1:T(8,128)}, u32[]{:S(2)}, u32[]{:S(2)}) collective-permute-start(f32[256,1024]{0,1:T(8,128)} %broadcast_select_fusion.1), channel_id=1, source_target_pairs={{0,64},{16,80},{32,96},{48,112},{1,65},{17,81},{33,97},{49,113},{2... | collective-permute-start | bytes 3145736 | tf_op jit(solution)/shard_map/ppermute | solution.py:22
  508.9 62.4 %copy-start.11 = (f32[256,1024]{0,1:T(8,128)}, f32[256,1024]{0,1:T(8,128)S(1)}, u32[]{:S(2)}) copy-start(f32[256,1024]{0,1:T(8,128)S(1)} %broadcast_select_fusion.3) | copy-start | bytes 3145732
  571.2 3.7 copy-start.13
  576.4 3.8 copy-start.29
  577.9 18.3 %copy-start.4 = (f32[128,3072]{1,0:T(8,128)}, f32[128,3072]{1,0:T(8,128)S(1)}, u32[]{:S(2)}) copy-start(f32[128,3072]{1,0:T(8,128)S(1)} %fusion.86) | copy-start | bytes 4718596
  580.2 19.6 %copy-start.27 = (s32[3]{0:T(128)S(1)}, s32[3]{0:T(128)}, u32[]{:S(2)}) copy-start(s32[3]{0:T(128)} %get-tuple-element.179) | copy-start | bytes 40
  580.3 19.6 %copy-start.28 = (s32[3]{0:T(128)S(1)}, s32[3]{0:T(128)}, u32[]{:S(2)}) copy-start(s32[3]{0:T(128)} %get-tuple-element.217) | copy-start | bytes 40
  596.2 43.8 %collective-permute-start.4 = (f32[3072,768]{0,1:T(8,128)}, f32[3072,768]{0,1:T(8,128)}, u32[]{:S(2)}, u32[]{:S(2)}) collective-permute-start(f32[3072,768]{0,1:T(8,128)} %get-tuple-element.250), channel_id=1, source_target_pairs={{0,1},{1,0},{2,3},{3,2},{4,5},{5,4},{6,7},{7,6},{8,9},{9,8},{10,11... | collective-permute-start | bytes 28311560 | tf_op jit(solution)/shard_map/ppermute | solution.py:32
  599.9 13.3 copy-start.24
  710.1 137.4 %collective-permute-start.5 = (f32[1536,1024]{1,0:T(8,128)}, f32[1536,1024]{1,0:T(8,128)}, u32[]{:S(2)}, u32[]{:S(2)}) collective-permute-start(f32[1536,1024]{1,0:T(8,128)} %get-tuple-element.226), channel_id=1, source_target_pairs={{0,16},{16,0},{32,48},{48,32},{64,80},{80,64},{96,112},{112,96},{1... | collective-permute-start | bytes 18874376 | tf_op jit(solution)/shard_map/ppermute | solution.py:32
  710.6 9.3 copy-start.26
  899.6 218.7 %all-reduce.14.cloned.1.call-start = ((), (), s32[]{:S(2)}) async-start(), calls=%async_computation.3 | async-start | bytes 2621440 | tf_op jit(solution)/shard_map/psum | solution.py:16
  1043.9 323.2 %all-reduce.16.cloned.1.call-start = ((), (), s32[]{:S(2)}) async-start(), calls=%async_computation.4 | async-start | bytes 4194304 | tf_op jit(solution)/shard_map/psum | solution.py:16
  1194.9 4.5 copy-start.14
  1200.5 12.6 copy-start.2
  1202.7 10.4 copy-start.8
  1218.0 3.8 copy-start.16
  1218.1 227.0 %all-reduce.18.cloned.1.call-start = ((), (), s32[]{:S(2)}) async-start(), calls=%async_computation.5 | async-start | bytes 2621440 | tf_op jit(solution)/shard_map/psum | solution.py:16
  1232.3 138.4 %copy-start.5 = (f32[128,3072]{1,0:T(8,128)S(1)}, f32[128,3072]{1,0:T(8,128)}, u32[]{:S(2)}) copy-start(f32[128,3072]{1,0:T(8,128)} %copy-done.4) | copy-start | bytes 4718596
  1373.5 4.2 copy-start.3
  1373.5 4.2 copy-start.9
  1380.9 102.9 %copy-start.25 = (pred[256]{0:T(512)(128)(4,1)S(1)}, pred[256]{0:T(512)(128)(4,1)}, u32[]{:S(2)}) copy-start(pred[256]{0:T(512)(128)(4,1)} %get-tuple-element.176) | copy-start | bytes 772
  1380.9 103.0 %copy-start.33 = (s32[2,2]{1,0:T(2,128)S(1)}, s32[2,2]{1,0:T(2,128)}, u32[]{:S(2)}) copy-start(s32[2,2]{1,0:T(2,128)} %get-tuple-element.479) | copy-start | bytes 52
  (14 other events, 29.4 us)
Sparse Core Ops, SparseCore 0:
  20.9 148.1 all-reduce.7
  307.7 146.3 all-reduce.9
  899.7 140.5 all-reduce.11
  1044.0 74.2 all-reduce.13
  1218.2 148.8 all-reduce.15
  1370.8 74.2 all-reduce.17
where the time goes:
time: 1570 us; the launch traced here: 1550 us
  waiting for transfers between devices  900 us (57%)
  other arithmetic  274 us (17%)
  matrix products  178 us (11%)
  local copies, waits for them, and re-layouts  166 us (11%)
  between operations  23.3 us (1%)
    psum x6, waiting for transfers between devices, spread(): return lax.psum(block, axis)  695 us
    another operation x27, other arithmetic, eliminate(): diag_factor = jnp.linalg.cholesky(joined[:, breadth:])  141 us
    ppermute x2, waiting for transfers between devices, partner(): return lax.ppermute(block, axis, route)  112 us
    ppermute x4, waiting for transfers between devices, from_behind(): return lax.ppermute(block, axis, route)  93 us
    another operation x6, other arithmetic, lower_solve(): lax.linalg.triangular_solve(diag_factor, right_side, left_side=True, lowe...  79.7 us
    dot_general x2, matrix products, spread_columns(): return jnp.einsum('rub,uq->rqb', blocks_view, selector, precision=highest)  56 us
    dot_general x4, matrix products, eliminate(): matrix = matrix - jnp.dot(row_part, col_part.T, precision=highest)  51.9 us
    unnamed x72, local copies, waits for them, and re-layouts  48.6 us
  transfers between devices with their start and end apart: 12, of which 11 were waited for; matrix products, arithmetic and copies ran while one was open for 7% of the time, Pallas kernels for 0%

commit v1 on v0

v1 whole, which is shorter than its diff:
```python
import functools

import jax
import jax.numpy as jnp
from jax import lax
from jax.experimental import pallas as pl
from jax.experimental.pallas import tpu as pltpu
from jax.sharding import PartitionSpec as P

NB = 256
PIV = 512
HI = lax.Precision.HIGHEST
MESH = pl.DeviceIdType.MESH
F32 = jnp.float32

def nt(a, b):
    return lax.dot_general(a, b, (((1,), (1,)), ((), ())), precision=HI, preferred_element_type=jnp.float32)

def nn(a, b):
    return lax.dot_general(a, b, (((1,), (0,)), ((), ())), precision=HI, preferred_element_type=jnp.float32)

def diag_inverse(work, s):
    tiles = [work[pl.ds(s + 8 * t, 8), pl.ds(s, 128)] for t in range(16)]
    rows8 = lax.broadcasted_iota(jnp.int32, (8, 128), 0)
    lanes = lax.broadcasted_iota(jnp.int32, (8, 128), 1)
    unit = [jnp.where(rows8 + 8 * t == lanes, 1.0, 0.0) for t in range(16)]
    scales = [jnp.zeros((8, 1), jnp.float32) for t in range(16)]
    for j in range(128):
        tj, i = j // 8, j % 8
        pivot = tiles[tj][i:i + 1, j:j + 1]
        inv = 1.0 / pivot
        row = tiles[tj][i:i + 1, :] * inv
        mrow = unit[tj][i:i + 1, :] * inv
        for t in range(tj, 16):
            col = tiles[t][:, j:j + 1]
            if t == tj:
                col = jnp.where(rows8[:, :1] > i, col, 0.0)
            tiles[t] = tiles[t] - col * row
            unit[t] = unit[t] - col * mrow
    out = []
    for t in range(16):
        d = jnp.sum(jnp.where(rows8 + 8 * t == lanes, tiles[t], 0.0), axis=1, keepdims=True)
        out.append(unit[t] * lax.rsqrt(d))
    return jnp.concatenate(out, axis=0)

def factor_inverse(work, low, inv, di):
    n = 512
    inv[...] = jnp.zeros_like(inv)
    low[...] = jnp.zeros_like(low)
    def step(b, _):
        s = pl.multiple_of(b * 128, 128)
        d = diag_inverse(work, s)
        panel = work[:, pl.ds(s, 128)]
        l21 = nt(panel, d)
        ids = lax.broadcasted_iota(jnp.int32, (n, 128), 0)
        l21 = jnp.where(ids >= s + 128, l21, 0.0)
        left = nn(low[pl.ds(s, 128), :], inv[...])
        inv[pl.ds(s, 128), :] = -nn(d, left)
        inv[pl.ds(s, 128), pl.ds(s, 128)] = d
        low[:, pl.ds(s, 128)] = l21
        work[...] = work[...] - nt(l21, l21)
        return 0
    lax.fori_loop(0, 4, step, 0)

def factor_kernel(a_ref, inv_ref, work, low):
    work[...] = a_ref[...]
    factor_inverse(work, low, inv_ref, None)


def leading_inverse(matrix):
    return pl.pallas_call(
        factor_kernel,
        grid=(1,),
        out_shape=jax.ShapeDtypeStruct((PIV, PIV), F32),
        in_specs=[pl.BlockSpec((PIV, PIV), lambda i: (0, 0))],
        out_specs=pl.BlockSpec((PIV, PIV), lambda i: (0, 0)),
        scratch_shapes=[pltpu.VMEM((PIV, PIV), F32)] * 2,
        compiler_params=pltpu.CompilerParams(vmem_limit_bytes=32 << 20),
        cost_estimate=pl.CostEstimate(flops=10**10, bytes_accessed=1 << 21, transcendentals=0),
        name="leading_inverse",
    )(matrix)


def send(src, dst, send_sem, recv_sem, **device):
    return pltpu.make_async_remote_copy(
        src_ref=src,
        dst_ref=dst,
        send_sem=send_sem,
        recv_sem=recv_sem,
        device_id=device,
        device_id_type=MESH,
    )


def panels_kernel(
    members,
    src,
    inverse,
    rows,
    cols,
    inv,
    row_put,
    row_got,
    row_out,
    row_in,
    row_over,
    col_put,
    col_got,
    col_out,
    col_in,
    col_over,
    inv_put,
    inv_got,
    inv_down,
    inv_down_got,
    inv_out,
    inv_in,
    inv_over,
    here,
):
    r = lax.axis_index("row")
    c = lax.axis_index("col")
    g, h = c // 2, c % 2
    parity = r % 2
    other = c + 1 - 2 * h
    mate = r + 1 - 2 * parity
    piece = rows.shape[3]
    strip = cols.shape[2] // 8
    own = parity if members == 2 else 0

    barrier = pltpu.get_barrier_semaphore()
    count = 0
    for d in range(1, 8):
        pl.semaphore_signal(barrier, 1, device_id={"row": (r + d) % 8}, device_id_type=MESH)
        count += 1
    for d in range(1, 16):
        pl.semaphore_signal(barrier, 1, device_id={"col": (c + d) % 16}, device_id_type=MESH)
        count += 1
        if members == 2:
            pl.semaphore_signal(
                barrier, 1, device_id={"row": mate, "col": (c + d) % 16}, device_id_type=MESH
            )
            count += 1
    pl.semaphore_wait(barrier, count)

    def row_piece(target_row, dest):
        start = (dest % 2 * 8 + dest // 2) * piece
        if members == 2:
            start = start + target_row % 2 * (16 * piece)
        return src.at[pl.ds(pl.multiple_of(start, 8), piece), pl.ds(0, PIV)]

    def col_strip(dest):
        return src.at[pl.ds(pl.multiple_of(dest * strip, 8), strip), :]

    def col_slot(half, k, dest):
        return cols.at[half, k, pl.ds(pl.multiple_of(dest * strip, 8), strip), :]

    def row_scatter(d, own_row):
        dest = (c + d) % 16
        target = r if own_row else mate
        return send(
            row_piece(target, dest),
            rows.at[own, dest % 2, dest // 2],
            row_put.at[0 if own_row else 1, d],
            row_got.at[own],
            row=target,
            col=dest,
        )

    def col_scatter(k, d):
        dest = (r + d) % 8
        return send(
            col_strip(dest), col_slot(h, k, dest), col_put.at[d], col_got.at[k], row=dest, col=c
        )

    def inv_scatter(k, d):
        dest = (c + d) % 16
        at = (dest % 2 * 8 + dest // 2) * 32
        return send(
            inverse.at[pl.ds(pl.multiple_of(at, 8), 32), :],
            inv.at[k, dest % 2, dest // 2],
            inv_put.at[d],
            inv_got.at[k],
            row=r,
            col=dest,
        )

    local_row = pltpu.make_async_copy(row_piece(r, c), rows.at[own, h, g], here.at[0])
    local_col = pltpu.make_async_copy(col_strip(r), col_slot(h, r, r), here.at[1])
    local_inv = pltpu.make_async_copy(inverse.at[pl.ds(0, 32), :], inv.at[r, 0, 0], here.at[2])

    @pl.when(r < members)
    def _():
        local_col.start()

        @pl.loop(1, 8)
        def _(d):
            col_scatter(r, d).start()

    @pl.when(c == 0)
    def _():
        local_row.start()

        @pl.loop(1, 16)
        def _(d):
            row_scatter(d, True).start()

        if members == 2:
            row_scatter(0, False).start()

            @pl.loop(1, 16)
            def _(d):
                row_scatter(d, False).start()

    @pl.when((r < members) & (c == 0))
    def _():
        local_inv.start()

        @pl.loop(1, 16)
        def _(d):
            inv_scatter(r, d).start()

    def col_gather(k, d):
        return send(
            col_slot(h, k, r),
            col_slot(h, k, r),
            col_out.at[k, d],
            col_in.at[k, r],
            row=(r + d) % 8,
            col=c,
        )

    def col_arrival(k, d):
        sender = (r + d) % 8
        return send(
            col_slot(h, k, sender),
            col_slot(h, k, sender),
            col_out.at[k, d],
            col_in.at[k, sender],
            row=sender,
            col=c,
        )

    def row_gather(k, d):
        return send(
            rows.at[k, h, g],
            rows.at[k, h, g],
            row_out.at[k, d],
            row_in.at[k, g],
            row=r,
            col=(g + d) % 8 * 2 + h,
        )

    def row_arrival(k, d):
        sender = (g + d) % 8
        return send(
            rows.at[k, h, sender],
            rows.at[k, h, sender],
            row_out.at[k, d],
            row_in.at[k, sender],
            row=r,
            col=sender * 2 + h,
        )

    def inv_column(k, d):
        return send(
            inv.at[k, h, g],
            inv.at[k, h, g],
            inv_down.at[d],
            inv_down_got.at[k],
            row=(r + d) % 8,
            col=c,
        )

    def inv_gather(k, d):
        return send(
            inv.at[k, h, g],
            inv.at[k, h, g],
            inv_out.at[k, d],
            inv_in.at[k, g],
            row=r,
            col=(g + d) % 8 * 2 + h,
        )

    def inv_arrival(k, d):
        sender = (g + d) % 8
        return send(
            inv.at[k, h, sender],
            inv.at[k, h, sender],
            inv_out.at[k, d],
            inv_in.at[k, sender],
            row=r,
            col=sender * 2 + h,
        )

    for k in range(members):

        @pl.when(r == k)
        def _():
            local_col.wait()

        @pl.when(r != k)
        def _():
            col_scatter(k, 1).wait_recv()

        @pl.loop(1, 8)
        def _(d):
            col_gather(k, d).start()

    for k in range(members):
        mine = (c == 0) & (own == k)

        @pl.when(mine)
        def _():
            local_row.wait()

        @pl.when(jnp.logical_not(mine))
        def _():
            send(
                rows.at[k, h, g], rows.at[k, h, g], row_put.at[0, 0], row_got.at[k], row=r, col=other
            ).wait_recv()

        @pl.loop(1, 8)
        def _(d):
            row_gather(k, d).start()

    for k in range(members):

        @pl.when((r == k) & (c == 0))
        def _():
            local_inv.wait()

        @pl.when((r == k) & (c != 0))
        def _():
            inv_scatter(k, 1).wait_recv()

        @pl.when(r == k)
        def _():
            @pl.loop(1, 8)
            def _(d):
                inv_column(k, d).start()

    for k in range(members):

        @pl.when(r != k)
        def _():
            inv_column(k, 1).wait_recv()

        @pl.loop(1, 8)
        def _(d):
            inv_gather(k, d).start()

    def cross(buffer, half, sems):
        return send(buffer, buffer, sems.at[0], sems.at[1], row=r, col=other)

    def col_cross(half):
        return cross(cols.at[half], half, col_over)

    for k in range(members):

        @pl.loop(1, 8)
        def _(d):
            col_arrival(k, d).wait_recv()

    if members == 2:
        col_cross(h).start()
    for k in range(members):

        @pl.loop(1, 8)
        def _(d):
            row_arrival(k, d).wait_recv()

        cross(rows.at[k, h], h, row_over.at[k]).start()
    for k in range(members):

        @pl.loop(1, 8)
        def _(d):
            inv_arrival(k, d).wait_recv()

        cross(inv.at[k, h], h, inv_over.at[k]).start()

    if members == 2:
        col_cross(1 - h).wait_recv()
        col_cross(h).wait_send()
    for k in range(members):
        cross(rows.at[k, 1 - h], h, row_over.at[k]).wait_recv()
        cross(rows.at[k, h], h, row_over.at[k]).wait_send()
        cross(inv.at[k, 1 - h], h, inv_over.at[k]).wait_recv()
        cross(inv.at[k, h], h, inv_over.at[k]).wait_send()

        @pl.loop(1, 8)
        def _(d):
            col_gather(k, d).wait_send()
            row_gather(k, d).wait_send()
            inv_gather(k, d).wait_send()

        @pl.when(r == k)
        def _():
            @pl.loop(1, 8)
            def _(d):
                col_scatter(k, d).wait_send()
                inv_column(k, d).wait_send()

        @pl.when((r == k) & (c == 0))
        def _():
            @pl.loop(1, 16)
            def _(d):
                inv_scatter(k, d).wait_send()

    @pl.when(c == 0)
    def _():
        @pl.loop(1, 16)
        def _(d):
            row_scatter(d, True).wait_send()

        if members == 2:

            @pl.loop(0, 16)
            def _(d):
                row_scatter(d, False).wait_send()


def share_panels(members, source, inverse, piece, collective_id):
    width = source.shape[1]
    dma = pltpu.SemaphoreType.DMA
    out_shape = (
        jax.ShapeDtypeStruct((members, 2, 8, piece, PIV), F32),
        jax.ShapeDtypeStruct((2, members, PIV, width), F32),
        jax.ShapeDtypeStruct((members, 2, 8, 32, PIV), F32),
    )
    scratch = [
        dma((2, 16)),
        dma((members,)),
        dma((members, 8)),
        dma((members, 8)),
        dma((members, 2)),
        dma((8,)),
        dma((members,)),
        dma((members, 8)),
        dma((members, 8)),
        dma((2,)),
        dma((16,)),
        dma((members,)),
        dma((8,)),
        dma((members,)),
        dma((members, 8)),
        dma((members, 8)),
        dma((members, 2)),
        dma((3,)),
    ]
    rows, cols, inv = pl.pallas_call(
        functools.partial(panels_kernel, members),
        out_shape=out_shape,
        in_specs=[pl.BlockSpec(memory_space=pl.ANY)] * 2,
        out_specs=[pl.BlockSpec(memory_space=pl.ANY)] * 3,
        scratch_shapes=scratch,
        compiler_params=pltpu.CompilerParams(collective_id=collective_id, has_side_effects=True),
        cost_estimate=pl.CostEstimate(flops=10**10, bytes_accessed=1 << 25, transcendentals=0),
        name="share_panels_%d" % members,
    )(source, inverse)
    return (
        rows.reshape(members, 16 * piece, PIV),
        cols,
        inv.reshape(members, PIV, PIV),
    )


def split(value):
    high = value.astype(jnp.bfloat16)
    return high, (value - high.astype(F32)).astype(jnp.bfloat16)


def dot3(left, right):
    (lh, ll), (rh, rl) = left, right

    def one(a, b):
        return jnp.dot(a, b, preferred_element_type=F32)

    return one(lh, rh) + (one(lh, rl) + one(ll, rh))


def assemble_kernel(
    info,
    rowi,
    rowv,
    colj,
    colv,
    parent,
    rows0,
    rows1,
    cols,
    inv,
    *rest,
):
    blocks = rest[:16]
    out, high, low = rest[16:]
    t = pl.program_id(0)
    half = info[1]

    @pl.when(t == 0)
    def _():
        for m in range(2):
            k = info[0] if m == 0 else 1 - info[0]
            for u in range(4):
                j = colj[m, u]
                at = pl.multiple_of(j % 3 * NB, NB)
                block = cols[j // 3, k, :, pl.ds(at, NB)]
                solved = nn(inv[k], block)
                solved = jnp.where(colv[m, u] > 0, solved, 0.0)
                sh, sl = split(solved)
                high[m, :, u * NB : (u + 1) * NB] = sh
                low[m, :, u * NB : (u + 1) * NB] = sl

    total = parent[...]
    for m in range(2):
        k = info[0] if m == 0 else 1 - info[0]
        panel = (rows0, rows1)[m]
        solved = nt(panel[0], inv[k])
        solved = jnp.where(rowv[m, t] > 0, solved, 0.0)
        total = total - dot3(split(solved), (high[m], low[m]))
        adds = []
        for u in range(4):
            mine, theirs = blocks[m * 8 + u], blocks[m * 8 + 4 + u]
            use = (rowv[m, t] > 0) & (colv[m, u] > 0)
            block = jnp.where(colj[m, u] // 3 == half, mine[...], theirs[...])
            adds.append(jnp.where(use, block, 0.0))
        total = total + jnp.concatenate(adds, axis=1)
    out[...] = total


def assemble(info, rowi, rowv, colj, colv, parent, rows, cols, inv, pieces):
    def panel_spec(m):
        def index(t, info, rowi, rowv, colj, colv):
            return (info[0] if m == 0 else 1 - info[0], rowi[m, t], 0)

        return pl.BlockSpec((1, NB, PIV), index)

    def block_spec(m, place, u, offset):
        def index(t, info, rowi, rowv, colj, colv):
            here = colj[m, u] // 3 == info[1]
            want = here if place == 0 else jnp.logical_not(here)
            row = rowi[m, t] + (info[0] * 6 if offset else 0)
            return (jnp.where(want, row, 0), jnp.where(want, colj[m, u] % 3, 0))

        return pl.BlockSpec((NB, NB), index)

    specs, operands = [], []
    for m in range(2):
        for place in range(2):
            for u in range(4):
                specs.append(block_spec(m, place, u, m == 0 and place == 0))
                operands.append(pieces[m][place])
    whole = pl.BlockSpec(memory_space=pltpu.VMEM)
    grid_spec = pltpu.PrefetchScalarGridSpec(
        num_scalar_prefetch=5,
        grid=(8,),
        in_specs=[
            pl.BlockSpec((NB, 1024), lambda t, *_: (t, 0)),
            panel_spec(0),
            panel_spec(1),
            whole,
            whole,
            *specs,
        ],
        out_specs=pl.BlockSpec((NB, 1024), lambda t, *_: (t, 0)),
        scratch_shapes=[pltpu.VMEM((2, PIV, 1024), jnp.bfloat16)] * 2,
    )
    return pl.pallas_call(
        assemble_kernel,
        grid_spec=grid_spec,
        out_shape=jax.ShapeDtypeStruct((2048, 1024), F32),
        compiler_params=pltpu.CompilerParams(vmem_limit_bytes=56 << 20),
        cost_estimate=pl.CostEstimate(flops=10**10, bytes_accessed=1 << 25, transcendentals=0),
        name="assemble",
    )(info, rowi, rowv, colj, colv, parent, rows, rows, cols, inv, *operands)


def finish_kernel(info, front, rows, cols, inv, out, high, low):
    t = pl.program_id(0)

    @pl.when(t == 0)
    def _():
        for u in range(4):
            span = slice(u * NB, (u + 1) * NB)
            sh, sl = split(nn(inv[...], cols[:, span]))
            high[:, span] = sh
            low[:, span] = sl

    solved = nt(rows[...], inv[...])
    total = front[...] - dot3(split(solved), (high[...], low[...]))
    in_pivots = (info[0] == 0) & (t < 2)
    wide = lax.broadcasted_iota(jnp.int32, total.shape, 0)
    total = jnp.where(in_pivots & (wide >= 0), 0.0, total)
    row_ids = t * NB + lax.broadcasted_iota(jnp.int32, solved.shape, 0)
    col_ids = lax.broadcasted_iota(jnp.int32, solved.shape, 1)
    factor = jnp.where(in_pivots & (col_ids > row_ids), 0.0, solved)
    lead = jnp.where((info[1] == 0) & (col_ids >= 0), factor, total[:, :PIV])
    out[:, :PIV] = lead
    out[:, PIV:] = total[:, PIV:]


def finish(info, front, rows, cols, inv):
    whole = pl.BlockSpec(memory_space=pltpu.VMEM)
    grid_spec = pltpu.PrefetchScalarGridSpec(
        num_scalar_prefetch=1,
        grid=(8,),
        in_specs=[
            pl.BlockSpec((NB, 1024), lambda t, *_: (t, 0)),
            pl.BlockSpec((NB, PIV), lambda t, *_: (t, 0)),
            whole,
            whole,
        ],
        out_specs=pl.BlockSpec((NB, 1024), lambda t, *_: (t, 0)),
        scratch_shapes=[pltpu.VMEM((PIV, 1024), jnp.bfloat16)] * 2,
    )
    return pl.pallas_call(
        finish_kernel,
        grid_spec=grid_spec,
        out_shape=jax.ShapeDtypeStruct((2048, 1024), F32),
        compiler_params=pltpu.CompilerParams(vmem_limit_bytes=56 << 20),
        cost_estimate=pl.CostEstimate(flops=10**10, bytes_accessed=1 << 25, transcendentals=0),
        name="finish",
    )(info, front, rows, cols, inv)


def inverse_map(targets, first, places, base):
    blocks = first + jnp.arange(6, dtype=jnp.int32)
    usable = blocks >= PIV // NB
    wanted = jnp.clip(blocks - PIV // NB, 0, targets.shape[0] - 1)
    known = jnp.arange(targets.shape[0], dtype=jnp.int32)
    target = jnp.sum(jnp.where(known[None, :] == wanted[:, None], targets[None, :], 0), axis=1)
    hit = usable[:, None] & (target[:, None] == places[None, :])
    index = jnp.sum(jnp.where(hit, jnp.arange(6, dtype=jnp.int32)[:, None], 0), axis=0)
    return index.astype(jnp.int32), jnp.any(hit, axis=0).astype(jnp.int32)


def local(children, parent, relay_map):
    r = lax.axis_index("row")
    c = lax.axis_index("col")
    parity = r % 2
    g, h = c // 2, c % 2
    pair_rows = [(i, i ^ 1) for i in range(8)]
    pair_cols = [(i, i ^ 1) for i in range(16)]

    kept = lax.dynamic_slice_in_dim(children, parity * 1536, 1536, 0)
    leaving = lax.dynamic_slice_in_dim(children, (1 - parity) * 1536, 1536, 0)
    received = lax.ppermute(leaving, "row", pair_rows)
    kept_over = lax.ppermute(kept, "col", pair_cols)

    inverse = leading_inverse(children)
    rows, cols, inv = share_panels(2, children, inverse, 96, 0)
    received_over = lax.ppermute(received, "col", pair_cols)

    row_places = r * 8 + jnp.arange(8, dtype=jnp.int32)
    col_places = c * 4 + jnp.arange(4, dtype=jnp.int32)
    own_map = jnp.where(parity == 0, relay_map[0], relay_map[1])
    other_map = jnp.where(parity == 0, relay_map[1], relay_map[0])
    own_r = inverse_map(own_map, r * 6, row_places, 0)
    other_r = inverse_map(other_map, r * 6, row_places, 0)
    own_c = inverse_map(own_map, g * 6, col_places, 0)
    other_c = inverse_map(other_map, g * 6, col_places, 0)
    rowi, rowv = (jnp.stack(pair) for pair in zip(own_r, other_r))
    colj, colv = (jnp.stack(pair) for pair in zip(own_c, other_c))
    info = jnp.stack([parity, h]).astype(jnp.int32)
    front = assemble(
        info,
        rowi,
        rowv,
        colj,
        colv,
        parent,
        rows,
        cols,
        inv,
        ((children, kept_over), (received, received_over)),
    )

    inv_part = lax.dynamic_slice_in_dim(inv, c * 32, 32, 1)
    factors = jnp.einsum("kic,kjc->kij", rows, inv_part, precision=HI)
    mine = lax.dynamic_index_in_dim(factors, parity, 0, keepdims=False)
    theirs = lax.dynamic_index_in_dim(factors, 1 - parity, 0, keepdims=False)
    mates = lax.ppermute(theirs, "row", pair_rows)
    child_factor = jnp.where(
        parity == 0, jnp.concatenate([mine, mates]), jnp.concatenate([mates, mine])
    )
    row_ids = r // 2 * 3072 + jnp.arange(3072, dtype=jnp.int32)
    col_ids = c * 32 + jnp.arange(32, dtype=jnp.int32)
    child_factor = jnp.where(row_ids[:, None] >= col_ids[None, :], child_factor, 0.0)

    inverse = leading_inverse(front)
    rows, cols, inv = share_panels(1, front, inverse, 128, 1)
    place = jnp.stack([r, c]).astype(jnp.int32)
    parent_out = finish(place, front, rows[0], lax.dynamic_index_in_dim(cols[:, 0], h, 0, False), inv[0])
    return parent_out, child_factor


def solution(mesh):
    return jax.shard_map(
        local,
        mesh=mesh,
        in_specs=(P("row", "col"), P("row", "col"), P()),
        out_specs=(P("row", "col"), P("row", "col")),
        check_vma=False,
    )
```

time: 1570 us -> 538 us (0.34)
  waiting for transfers between devices: 900 us -> 103 us
  Pallas kernels: 0 us -> 392 us
  other arithmetic: 274 us -> 4.46 us
  matrix products: 178 us -> 7.87 us
  local copies, waits for them, and re-layouts: 166 us -> 15.5 us
  between operations: 23.3 us -> 0.87 us
    psum x6 -> x0, waiting for transfers between devices: 695 us -> none  [spread(): return lax.psum(block, axis)]
    pallas_call x0 -> x6, Pallas kernels: none -> 392 us  [the longest x2 215 us: share_panels(): pl.pallas_call(functools.partial(panels_kernel, members), out_shape=out_s...]
    another operation x33 -> x5, other arithmetic: 221 us -> 2.8 us  [the longest x2 1.08 us: local(): colj, colv = (jnp.stack(pair) for pair in zip(own_c, other_c))]
    dot_general x8 -> x1, matrix products: 140 us -> 7.87 us  [local(): factors = jnp.einsum('kic,kjc->kij', rows, inv_part, precision=HI)]
    ppermute x6 -> x4, waiting for transfers between devices: 205 us -> 103 us  [the longest x1 101 us: local(): received = lax.ppermute(leaving, 'row', pair_rows)]
    unnamed x72 -> x10, local copies, waits for them, and re-layouts: 48.6 us -> 5.33 us
    reshape x3 -> x0, local copies, waits for them, and re-layouts: 42.2 us -> none  [the longest x1 15.7 us: local(): widened = (kept + arrived).reshape(2, half_height, parent_width)]
    another operation x32 -> x0, matrix products: 38.2 us -> none  [the longest x24 34.2 us: lower_solve(): lax.linalg.triangular_solve(diag_factor, right_side, left_side=True, lowe...]
  transfers between devices with their start and end apart: 12 -> 4, of which waited for: 11 -> 2; matrix products, arithmetic and copies ran while one was open for 7% -> 2% of each run, Pallas kernels for 0% -> 31%
where the time goes in v1:
time: 538 us; the launch traced here: 528 us
  Pallas kernels  392 us (73%)
  waiting for transfers between devices  103 us (19%)
  local copies, waits for them, and re-layouts  15.5 us (3%)
  matrix products  7.87 us (1%)
    pallas_call x2, Pallas kernels, share_panels(): pl.pallas_call(functools.partial(panels_kernel, members), out_shape=out_s...  215 us
    pallas_call x2, Pallas kernels, leading_inverse(): pl.pallas_call(factor_kernel, grid=(1,), out_shape=jax.ShapeDtypeStruct((...  104 us
    ppermute x1, waiting for transfers between devices, local(): received = lax.ppermute(leaving, 'row', pair_rows)  101 us
    pallas_call x1, Pallas kernels, assemble(): pl.pallas_call(assemble_kernel, grid_spec=grid_spec, out_shape=jax.ShapeD...  49.1 us
    pallas_call x1, Pallas kernels, finish(): pl.pallas_call(finish_kernel, grid_spec=grid_spec, out_shape=jax.ShapeDty...  24 us
  transfers between devices with their start and end apart: 4, of which 2 were waited for; matrix products, arithmetic and copies ran while one was open for 2% of the time, Pallas kernels for 31%

profile of v1, /device:TPU:57, one launch (start us, length us, event | category | flops | bytes accessed | tf_op | source)
XLA Modules:
  0.0 527.6 jit_solution(10570513167002027345)
XLA Ops:
  0.7 0.0 copy-start
  0.7 7.0 %constant_dynamic-slice_fusion = (f32[1536,768]{1,0:T(8,128)S(1)}, f32[1536,768]{1,0:T(8,128)}) fusion(f32[3072,768]{1,0:T(8,128)} %rest_3_.1, s32[]{:T(128)S(6)} %select_n.106, s32[]{:T(128)S(6)} %select_n.105), kind=kLoop, calls=%fused_computation.27 | loop fusion | bytes 18874376 | tf_op jit(solution)/shard_map/dynamic_slice | solution.py:646
  7.6 0.5 collective-permute-start.1
  8.1 1.0 collective-permute-start
  9.0 101.4 %collective-permute-done.1.rest_8_.rest_9_.rest_10_.rest_11_ = f32[1536,768]{1,0:T(8,128)} collective-permute-done((f32[1536,768]{1,0:T(8,128)S(1)}, f32[1536,768]{1,0:T(8,128)}, u32[]{:S(2)}, u32[]{:S(2)}) %collective-permute-start.1) | collective-permute-done | bytes 4718624 | tf_op jit(solution)/shard_map/ppermute | solution.py:647
  110.4 1.5 collective-permute-start.2
  111.9 51.8 %leading_inverse.2.inverse = f32[512,512]{1,0:T(8,128)S(1)} custom-call(f32[3072,768]{1,0:T(8,128)S(1)} %copy-done), custom_call_target="tpu_custom_call" | custom-call | flops 10000000000 | bytes 2097152 | tf_op jit(solution)/shard_map/leading_inverse/pallas_call | solution.py:71
  163.8 1.0 copy-done.2
  164.8 113.1 %share_panels_2.1 = (f32[2,2,8,96,512]{4,3,2,1,0:T(8,128)}, f32[2,2,512,768]{3,2,1,0:T(8,128)}, f32[2,2,8,32,512]{4,3,2,1,0:T(8,128)}) custom-call(f32[3072,768]{1,0:T(8,128)} %rest_3_.1, f32[512,512]{1,0:T(8,128)} %copy-done.2), custom_call_target="tpu_custom_call" | custom-call | flops 10000000000 | bytes 33554432 | tf_op jit(solution)/shard_map/share_panels_2/pallas_call | solution.py:451
  277.9 0.0 copy-start.4
  277.9 7.9 %fusion.1 = f32[2,1536,32]{1,2,0:T(8,128)S(1)} fusion(f32[2,1536,512]{2,1,0:T(8,128)} %bitcast.27, f32[2,512,512]{2,1,0:T(8,128)} %bitcast.30, s32[]{:T(128)S(6)} %select_n.110), kind=kOutput, calls=%fused_computation.5 | convolution fusion | flops 603979776 | bytes 6815748 | tf_op jit(solution)/shard_map/kic,kjc->kij/dot_general | solution.py:679
  285.8 0.3 collective-permute-start.3
  286.2 0.2 select_reduce_fusion.1
  286.4 0.1 select_reduce_fusion.4
  286.5 0.5 pad_add_fusion.rowi
  287.1 0.1 fusion.4
  287.2 0.5 add_convert_fusion.rowv
  287.7 0.2 select_reduce_fusion.7
  287.9 0.6 pad_add_fusion.1.colj
  288.4 0.2 fusion.6
  288.6 0.5 add_convert_fusion.1.colv
  289.1 0.6 pad_add_fusion.2
  289.8 2.1 collective-permute-done.3
  291.9 0.8 fusion
  292.8 49.1 %assemble.1.a_ref.src.front = f32[2048,1024]{1,0:T(8,128)} custom-call(s32[2]{0:T(128)} %get-tuple-element.33.info, s32[2,8]{1,0:T(2,128)} %pad_add_fusion.rowi, s32[2,8]{1,0:T(2,128)} %add_convert_fusion.rowv, s32[2,4]{1,0:T(2,128)} %pad_add_fusion.1.colj, s32[2,4]{1,0:T(2,128)} %add_convert_fusion.1.colv, f32[2048,1024]{1,0:T(8,128)} %parent.1, ...), custom_call_target="tpu_custom_call" | custom-call | flops 10000000000 | bytes 33554432 | tf_op jit(solution)/shard_map/assemble/pallas_call | solution.py:568
  341.9 3.4 copy-done.1
  345.3 52.0 %leading_inverse.3.inverse = f32[512,512]{1,0:T(8,128)S(1)} custom-call(f32[2048,1024]{1,0:T(8,128)S(1)} %copy-done.1), custom_call_target="tpu_custom_call" | custom-call | flops 10000000000 | bytes 2097152 | tf_op jit(solution)/shard_map/leading_inverse/pallas_call | solution.py:71
  397.3 0.0 copy-start.3
  397.3 1.0 copy-done.3
  398.3 102.2 %share_panels_1.1 = (f32[1,2,8,128,512]{4,3,2,1,0:T(8,128)}, f32[2,1,512,1024]{3,2,1,0:T(8,128)}, f32[1,2,8,32,512]{4,3,2,1,0:T(8,128)}) custom-call(f32[2048,1024]{1,0:T(8,128)} %assemble.1.a_ref.src.front, f32[512,512]{1,0:T(8,128)} %copy-done.3), custom_call_target="tpu_custom_call" | custom-call | flops 10000000000 | bytes 33554432 | tf_op jit(solution)/shard_map/share_panels_1/pallas_call | solution.py:451
  500.4 3.2 dynamic-slice_bitcast_fusion.cols
  503.6 24.0 %finish.1 = f32[2048,1024]{1,0:T(8,128)} custom-call(s32[2]{0:T(128)} %get-tuple-element.32.info, f32[2048,1024]{1,0:T(8,128)} %assemble.1.a_ref.src.front, f32[2048,512]{1,0:T(8,128)} %bitcast.40, f32[512,1024]{1,0:T(8,128)} %dynamic-slice_bitcast_fusion.cols, f32[512,512]{1,0:T(8,128)} %bitcast.41), custom_call_target="tpu_custom_call" | custom-call | flops 10000000000 | bytes 33554432 | tf_op jit(solution)/shard_map/finish/pallas_call | solution.py:616
  (15 shorter events, 0.1 us)
Async XLA Ops:
  0.7 111.3 %copy-start = (f32[3072,768]{1,0:T(8,128)S(1)}, f32[3072,768]{1,0:T(8,128)}, u32[]{:S(2)}) copy-start(f32[3072,768]{1,0:T(8,128)} %rest_3_.1) | copy-start | bytes 28311556
  7.6 102.8 %collective-permute-start.1 = (f32[1536,768]{1,0:T(8,128)S(1)}, f32[1536,768]{1,0:T(8,128)}, u32[]{:S(2)}, u32[]{:S(2)}) collective-permute-start(f32[1536,768]{1,0:T(8,128)S(1)} %get-tuple-element.26), channel_id=1, source_target_pairs={{0,16},{16,0},{32,48},{48,32},{64,80},{80,64},{96,112},{112,96},{1... | collective-permute-start | bytes 14155784 | tf_op jit(solution)/shard_map/ppermute | solution.py:647
  8.1 284.7 %collective-permute-start = (f32[1536,768]{1,0:T(8,128)}, f32[1536,768]{1,0:T(8,128)}, u32[]{:S(2)}, u32[]{:S(2)}) collective-permute-start(f32[1536,768]{1,0:T(8,128)} %get-tuple-element.27), channel_id=1, source_target_pairs={{0,1},{1,0},{2,3},{3,2},{4,5},{5,4},{6,7},{7,6},{8,9},{9,8},{10,11... | collective-permute-start | bytes 14155784 | tf_op jit(solution)/shard_map/ppermute | solution.py:648
  110.4 182.4 %collective-permute-start.2 = (f32[1536,768]{1,0:T(8,128)}, f32[1536,768]{1,0:T(8,128)}, u32[]{:S(2)}, u32[]{:S(2)}) collective-permute-start(f32[1536,768]{1,0:T(8,128)} %collective-permute-done.1.rest_8_.rest_9_.rest_10_.rest_11_), channel_id=1, source_target_pairs={{0,1},{1,0},{2,3},{3,2},{4,5},{5,4},{6,7},{7,6},{8,9},{9,8},{10,11... | collective-permute-start | bytes 14155784 | tf_op jit(solution)/shard_map/ppermute | solution.py:652
  163.8 1.0 copy-start.2
  277.9 8.3 %copy-start.4 = (s32[2,46]{1,0:T(2,128)S(1)}, s32[2,46]{1,0:T(2,128)}, u32[]{:S(2)}) copy-start(s32[2,46]{1,0:T(2,128)} %param.5) | copy-start | bytes 1108
  285.8 6.1 %collective-permute-start.3 = (f32[1536,32]{0,1:T(8,128)S(1)}, f32[1536,32]{0,1:T(8,128)S(1)}, u32[]{:S(2)}, u32[]{:S(2)}) collective-permute-start(f32[1536,32]{0,1:T(8,128)S(1)} %get-tuple-element.29), channel_id=1, source_target_pairs={{0,16},{16,0},{32,48},{48,32},{64,80},{80,64},{96,112},{112,96},{1... | collective-permute-start | bytes 589832 | tf_op jit(solution)/shard_map/ppermute | solution.py:682
  341.9 3.4 copy-start.1
  397.3 1.0 copy-start.3

commit v2 on v1

v2 whole, which is shorter than its diff:
```python
import jax
import jax.numpy as jnp
from jax import lax
from jax.experimental import pallas as pl
from jax.experimental.pallas import tpu as pltpu
from jax.sharding import PartitionSpec as P

NB = 256
PIV = 512
HI = lax.Precision.HIGHEST
MESH = pl.DeviceIdType.MESH
F32 = jnp.float32


def nt(a, b):
    return lax.dot_general(a, b, (((1,), (1,)), ((), ())), precision=HI, preferred_element_type=jnp.float32)

def nn(a, b):
    return lax.dot_general(a, b, (((1,), (0,)), ((), ())), precision=HI, preferred_element_type=jnp.float32)

def diag_inverse(work, s):
    tiles = [work[pl.ds(s + 8 * t, 8), pl.ds(s, 128)] for t in range(16)]
    rows8 = lax.broadcasted_iota(jnp.int32, (8, 128), 0)
    lanes = lax.broadcasted_iota(jnp.int32, (8, 128), 1)
    unit = [jnp.where(rows8 + 8 * t == lanes, 1.0, 0.0) for t in range(16)]
    scales = [jnp.zeros((8, 1), jnp.float32) for t in range(16)]
    for j in range(128):
        tj, i = j // 8, j % 8
        pivot = tiles[tj][i:i + 1, j:j + 1]
        inv = 1.0 / pivot
        row = tiles[tj][i:i + 1, :] * inv
        mrow = unit[tj][i:i + 1, :] * inv
        for t in range(tj, 16):
            col = tiles[t][:, j:j + 1]
            if t == tj:
                col = jnp.where(rows8[:, :1] > i, col, 0.0)
            tiles[t] = tiles[t] - col * row
            unit[t] = unit[t] - col * mrow
    out = []
    for t in range(16):
        d = jnp.sum(jnp.where(rows8 + 8 * t == lanes, tiles[t], 0.0), axis=1, keepdims=True)
        out.append(unit[t] * lax.rsqrt(d))
    return jnp.concatenate(out, axis=0)

def start_factor(low, inv):
    inv[...] = jnp.zeros_like(inv)
    low[...] = jnp.zeros_like(low)


def factor_step(b, work, low, inv):
    s = pl.multiple_of(b * 128, 128)
    span = pl.ds(s, 128)
    d = diag_inverse(work, s)
    ids = lax.broadcasted_iota(jnp.int32, (PIV, 128), 0)
    beneath = jnp.where(ids >= s + 128, nt(work[:, span], d), 0.0)
    left = nn(low[span, :], inv[...])
    inv[span, :] = -nn(d, left)
    inv[span, span] = d
    low[:, span] = beneath
    work[...] = work[...] - nt(beneath, beneath)


def send(src, dst, send_sem, recv_sem, **device):
    return pltpu.make_async_remote_copy(
        src_ref=src,
        dst_ref=dst,
        send_sem=send_sem,
        recv_sem=recv_sem,
        device_id=device,
        device_id_type=MESH,
    )


def share_kernel(members, moves, *refs):
    src = refs[0]
    refs = refs[1:]
    extra_in, refs = refs[: moves.inputs], refs[moves.inputs :]
    (cols, rows, inv), refs = refs[:3], refs[3:]
    extra_out, refs = refs[: moves.outputs], refs[moves.outputs :]
    work, low, made, diag_sem, here, *sems = refs
    (col_put, col_got, col_out, col_in, col_over) = sems[:5]
    (row_put, row_got, row_out, row_in, row_over) = sems[5:10]
    (inv_put, inv_got, inv_down, inv_down_got, inv_out, inv_in, inv_over) = sems[10:17]
    move_sems = sems[17:]

    r = lax.axis_index("row")
    c = lax.axis_index("col")
    g, h = c // 2, c % 2
    other = c + 1 - 2 * h
    mate = r + 1 - 2 * (r % 2)
    strip = PIV // 8
    giver = r < members
    root = giver & (c == 0)
    home = giver & (g == r)

    barrier = pltpu.get_barrier_semaphore()
    for d in range(1, 8):
        pl.semaphore_signal(barrier, 1, device_id={"row": (r + d) % 8}, device_id_type=MESH)
    for d in range(1, 16):
        pl.semaphore_signal(barrier, 1, device_id={"col": (c + d) % 16}, device_id_type=MESH)
    for k in range(members):

        @pl.when(jnp.logical_not((r == k) & (g == r)))
        def _():
            pl.semaphore_signal(
                barrier, 1, device_id={"row": k, "col": 2 * r + h}, device_id_type=MESH
            )

    @pl.when(giver)
    def _():
        for d in range(8):

            @pl.when(jnp.logical_not((g == r) & (g == d)))
            def _():
                pl.semaphore_signal(
                    barrier, 1, device_id={"row": g, "col": 2 * d + h}, device_id_type=MESH
                )

    count = 22 + members + jnp.where(giver, 8, 0) - jnp.where(home, 2, 0)
    pl.semaphore_wait(barrier, count)

    def part(index):
        return pl.ds(pl.multiple_of(index * strip, strip), strip)

    def slot(buffer, k, index, half=None):
        return buffer.at[h if half is None else half, k, part(index), :]

    def col_scatter(k, d):
        dest = (r + d) % 8
        return send(
            src.at[part(dest), :],
            slot(cols, k, dest),
            col_put.at[d],
            col_got.at[k],
            row=dest,
            col=c,
        )

    def row_scatter(k, dest):
        return send(
            src.at[part(dest), :],
            slot(rows, k, dest),
            row_put.at[dest],
            row_got.at[k],
            row=g,
            col=2 * dest + h,
        )

    def row_taken(k):
        return send(
            slot(rows, k, g), slot(rows, k, g), row_put.at[0], row_got.at[k], row=r, col=other
        )

    def inv_scatter(k, d):
        dest = (c + d) % 16
        at = (dest % 2 * 8 + dest // 2) * 32
        return send(
            made.at[pl.ds(pl.multiple_of(at, 32), 32), :],
            inv.at[k, dest % 2, dest // 2],
            inv_put.at[d],
            inv_got.at[k],
            row=r,
            col=dest,
        )

    local_diag = pltpu.make_async_copy(src.at[pl.ds(0, PIV), pl.ds(0, PIV)], work, diag_sem.at[0])
    local_col = pltpu.make_async_copy(src.at[part(r), :], slot(cols, r, r), here.at[1])
    local_row = pltpu.make_async_copy(src.at[part(g), :], slot(rows, r, g), here.at[0])
    local_inv = pltpu.make_async_copy(made.at[pl.ds(0, 32), :], inv.at[r, 0, 0], here.at[2])

    @pl.when(root)
    def _():
        local_diag.start()

    @pl.when(giver)
    def _():
        local_col.start()

        @pl.loop(1, 8)
        def _(d):
            col_scatter(r, d).start()

        @pl.loop(0, 8)
        def _(d):
            @pl.when(jnp.logical_not((g == r) & (g == d)))
            def _():
                row_scatter(r, d).start()

        @pl.when(home)
        def _():
            local_row.start()

    def block_move(index, relay=False):
        return moves.copy(index, relay, extra_in, extra_out, move_sems, send, r, c, h, mate, other)

    for index in range(moves.count):
        block_move(index).start()

    @pl.when(root)
    def _():
        local_diag.wait()
        start_factor(low, made)
        factor_step(0, work, low, made)

    def col_gather(k, d, sender=None):
        at = r if sender is None else sender
        return send(
            slot(cols, k, at),
            slot(cols, k, at),
            col_out.at[k, d],
            col_in.at[k, at],
            row=(r + d) % 8,
            col=c,
        )

    def row_gather(k, d, sender=None):
        at = g if sender is None else sender
        return send(
            slot(rows, k, at),
            slot(rows, k, at),
            row_out.at[k, d],
            row_in.at[k, at],
            row=r,
            col=(g + d) % 8 * 2 + h,
        )

    def inv_column(k, d):
        return send(
            inv.at[k, h, g],
            inv.at[k, h, g],
            inv_down.at[d],
            inv_down_got.at[k],
            row=(r + d) % 8,
            col=c,
        )

    def inv_gather(k, d, sender=None):
        at = g if sender is None else sender
        return send(
            inv.at[k, h, at],
            inv.at[k, h, at],
            inv_out.at[k, d],
            inv_in.at[k, at],
            row=r,
            col=(g + d) % 8 * 2 + h,
        )

    for k in range(members):

        @pl.when(r == k)
        def _():
            local_col.wait()

        @pl.when(r != k)
        def _():
            col_scatter(k, 1).wait_recv()

        @pl.loop(1, 8)
        def _(d):
            col_gather(k, d).start()

        @pl.when((r == k) & (g == r))
        def _():
            local_row.wait()

        @pl.when(jnp.logical_not((r == k) & (g == r)))
        def _():
            row_taken(k).wait_recv()

        @pl.loop(1, 8)
        def _(d):
            row_gather(k, d).start()

    @pl.when(root)
    def _():
        @pl.loop(1, 4)
        def _(b):
            factor_step(b, work, low, made)

        local_inv.start()

        @pl.loop(1, 16)
        def _(d):
            inv_scatter(r, d).start()

        local_inv.wait()

    def cross(buffer, sems):
        return send(buffer, buffer, sems.at[0], sems.at[1], row=r, col=other)

    if members == 2:
        for k in range(members):

            @pl.loop(1, 8)
            def _(d):
                col_gather(k, d, (r + d) % 8).wait_recv()

        cross(cols.at[h], col_over).start()
    for k in range(members):

        @pl.loop(1, 8)
        def _(d):
            row_gather(k, d, (g + d) % 8).wait_recv()

    cross(rows.at[h], row_over).start()

    for k in range(members):

        @pl.when((r == k) & (c != 0))
        def _():
            inv_scatter(k, 1).wait_recv()

        @pl.when(r == k)
        def _():
            @pl.loop(1, 8)
            def _(d):
                inv_column(k, d).start()

    for k in range(members):

        @pl.when(r != k)
        def _():
            inv_column(k, 1).wait_recv()

        @pl.loop(1, 8)
        def _(d):
            inv_gather(k, d).start()

    for index in range(moves.relayed):
        block_move(index).wait_recv()
        block_move(index, True).start()

    for k in range(members):

        @pl.loop(1, 8)
        def _(d):
            inv_gather(k, d, (g + d) % 8).wait_recv()

        cross(inv.at[k, h], inv_over.at[k]).start()

    if members == 1:

        @pl.loop(1, 8)
        def _(d):
            col_gather(0, d, (r + d) % 8).wait_recv()

    if members == 2:
        cross(cols.at[1 - h], col_over).wait_recv()
        cross(cols.at[h], col_over).wait_send()
    cross(rows.at[1 - h], row_over).wait_recv()
    cross(rows.at[h], row_over).wait_send()
    for index in range(moves.count):
        if index >= moves.relayed:
            block_move(index).wait_recv()
        block_move(index).wait_send()
        if index < moves.relayed:
            block_move(index, True).wait()
    for k in range(members):
        cross(inv.at[k, 1 - h], inv_over.at[k]).wait_recv()
        cross(inv.at[k, h], inv_over.at[k]).wait_send()

        @pl.loop(1, 8)
        def _(d):
            col_gather(k, d).wait_send()
            row_gather(k, d).wait_send()
            inv_gather(k, d).wait_send()

        @pl.when(r == k)
        def _():
            @pl.loop(1, 8)
            def _(d):
                col_scatter(k, d).wait_send()
                inv_column(k, d).wait_send()

            @pl.loop(0, 8)
            def _(d):
                @pl.when(jnp.logical_not((g == r) & (g == d)))
                def _():
                    row_scatter(k, d).wait_send()

        @pl.when((r == k) & (c == 0))
        def _():
            @pl.loop(1, 16)
            def _(d):
                inv_scatter(k, d).wait_send()


class EarlyMoves:
    inputs, outputs = 0, 2
    relayed = 4
    count = 5

    def copy(self, index, relay, ins, outs, sems, send, r, c, h, mate, other):
        (got, kept), (put_sem, got_sem, over_put, over_got) = outs, sems
        src = self.src
        if index == 4:
            rows = pl.ds(pl.multiple_of(r % 2 * 1536, NB), 1536)
            return send(src.at[rows, :], kept, put_sem.at[4], got_sem.at[4], row=r, col=other)
        if relay:
            block = got.at[h, pl.ds(index * NB, NB), :]
            return send(block, block, over_put.at[index], over_got.at[index], row=r, col=other)
        rows = pl.ds(pl.multiple_of((1 - r % 2) * 1536 + (index + 2) * NB, NB), NB)
        return send(
            src.at[rows, :],
            got.at[h, pl.ds(index * NB, NB), :],
            put_sem.at[index],
            got_sem.at[index],
            row=mate,
            col=c,
        )


class LateMoves:
    inputs, outputs = 2, 2
    relayed = 2
    count = 3

    def copy(self, index, relay, ins, outs, sems, send, r, c, h, mate, other):
        (children, factors), (got, mates), (put_sem, got_sem, over_put, over_got) = ins, outs, sems
        if index == 2:
            return send(
                factors.at[1 - r % 2], mates, put_sem.at[2], got_sem.at[2], row=mate, col=c
            )
        if relay:
            block = got.at[h, pl.ds(index * NB, NB), :]
            return send(block, block, over_put.at[index], over_got.at[index], row=r, col=other)
        rows = pl.ds(pl.multiple_of((1 - r % 2) * 1536 + index * NB, NB), NB)
        return send(
            children.at[rows, :],
            got.at[h, pl.ds(index * NB, NB), :],
            put_sem.at[index],
            got_sem.at[index],
            row=mate,
            col=c,
        )


def share(members, source, extras, moves, extra_shapes, collective_id):
    width = source.shape[1]
    dma = pltpu.SemaphoreType.DMA
    panel = jax.ShapeDtypeStruct((2, members, PIV, width), F32)
    out_shape = (panel, panel, jax.ShapeDtypeStruct((members, 2, 8, 32, PIV), F32), *extra_shapes)
    group = [dma((8,)), dma((members,)), dma((members, 8)), dma((members, 8)), dma((2,))]
    scratch = [
        pltpu.VMEM((PIV, PIV), F32),
        pltpu.VMEM((PIV, PIV), F32),
        pltpu.VMEM((PIV, PIV), F32),
        dma((1,)),
        dma((3,)),
        *group,
        *group,
        dma((16,)),
        dma((members,)),
        dma((8,)),
        dma((members,)),
        dma((members, 8)),
        dma((members, 8)),
        dma((members, 2)),
        dma((moves.count,)),
        dma((moves.count,)),
        dma((moves.relayed,)),
        dma((moves.relayed,)),
    ]

    def kernel(*refs):
        if members == 2:
            moves.src = refs[0]
        share_kernel(members, moves, *refs)

    cols, rows, inv, *extra = pl.pallas_call(
        kernel,
        out_shape=out_shape,
        in_specs=[pl.BlockSpec(memory_space=pl.ANY)] * (1 + len(extras)),
        out_specs=[pl.BlockSpec(memory_space=pl.ANY)] * len(out_shape),
        scratch_shapes=scratch,
        compiler_params=pltpu.CompilerParams(
            collective_id=collective_id, has_side_effects=True, vmem_limit_bytes=56 << 20
        ),
        cost_estimate=pl.CostEstimate(flops=10**10, bytes_accessed=1 << 25, transcendentals=0),
        name="share_panels_%d" % members,
    )(source, *extras)
    return cols, rows, inv.reshape(members, PIV, PIV), extra


def split(value):
    high = value.astype(jnp.bfloat16)
    return high, (value - high.astype(F32)).astype(jnp.bfloat16)


def dot3(left, right):
    (lh, ll), (rh, rl) = left, right

    def one(a, b):
        return jnp.dot(a, b, preferred_element_type=F32)

    return one(lh, rh) + (one(lh, rl) + one(ll, rh))


def column_block(panels, k, block):
    at = pl.multiple_of(block % 3 * NB, NB)
    return panels[block // 3, k, :, pl.ds(at, NB)]


def update_blocks(t, info, rowi, rowv, colj, colv, blocks):
    total = None
    for m in range(2):
        adds = []
        for u in range(4):
            first, second = blocks[m * 8 + u], blocks[m * 8 + 4 + u]
            use = (rowv[m, t] > 0) & (colv[m, u] > 0)
            if m == 0:
                block = jnp.where(colj[m, u] // 3 == info[1], first[...], second[...])
            else:
                block = jnp.where(rowi[m, t] >= 2, first[0], second[0])
            adds.append(jnp.where(use, block, 0.0))
        sum_m = jnp.concatenate(adds, axis=1)
        total = sum_m if total is None else total + sum_m
    return total


def block_specs():
    def own(u, place):
        def index(t, info, rowi, rowv, colj, colv):
            here = colj[0, u] // 3 == info[1]
            want = here if place == 0 else jnp.logical_not(here)
            row = rowi[0, t] + (info[0] * 6 if place == 0 else 0)
            return (jnp.where(want, row, 0), jnp.where(want, colj[0, u] % 3, 0))

        return pl.BlockSpec((NB, NB), index)

    def mates(u, place):
        def index(t, info, rowi, rowv, colj, colv):
            late = rowi[1, t] < 2
            want = jnp.logical_not(late) if place == 0 else late
            row = rowi[1, t] - (2 if place == 0 else 0)
            core = colj[1, u] // 3
            return (core, jnp.where(want, row, 0), jnp.where(want, colj[1, u] % 3, 0))

        return pl.BlockSpec((1, NB, NB), index)

    return [own(u, place) for place in range(2) for u in range(4)] + [
        mates(u, place) for place in range(2) for u in range(4)
    ]


def panel_kernel(info, rowi, rowv, colj, colv, parent, rows, cols, inv, inv_part, *rest):
    blocks, (front, high, low, factors), (inv_h, inv_l) = rest[:16], rest[16:20], rest[20:]
    t = pl.program_id(0)

    @pl.when(t == 0)
    def _():
        for k in range(2):
            inv_h[k], inv_l[k] = split(inv[k])
        for m in range(2):
            k = info[0] if m == 0 else 1 - info[0]
            for u in range(4):
                block = split(column_block(cols, k, colj[m, u]))
                solved = dot3((inv_h[k], inv_l[k]), block)
                solved = jnp.where(colv[m, u] > 0, solved, 0.0)
                sh, sl = split(solved)
                high[m, :, u * NB : (u + 1) * NB] = sh
                low[m, :, u * NB : (u + 1) * NB] = sl
        for k in range(2):
            part = split(inv_part[k])
            for half in range(2):
                factors[k, :, half * 768 : (half + 1) * 768] = dot3(part, split(rows[half, k]))

    total = parent[...] + update_blocks(t, info, rowi, rowv, colj, colv, blocks)
    for m in range(2):
        k = info[0] if m == 0 else 1 - info[0]
        block = split(column_block(rows, k, rowi[m, t]))
        solved = dot3((inv_h[k], inv_l[k]), block)
        solved = jnp.where(rowv[m, t] > 0, solved, 0.0)
        total = total - dot3(split(solved.T), (high[m], low[m]))
    front[...] = total


def panel_front(maps, parent, rows, cols, inv, inv_part, pieces):
    whole = pl.BlockSpec(memory_space=pltpu.VMEM)
    full = lambda shape: pl.BlockSpec(shape, lambda t, *_: (0,) * len(shape))
    grid_spec = pltpu.PrefetchScalarGridSpec(
        num_scalar_prefetch=5,
        grid=(2,),
        in_specs=[
            pl.BlockSpec((NB, 1024), lambda t, *_: (t, 0)),
            whole,
            whole,
            whole,
            whole,
            *block_specs(),
        ],
        out_specs=[
            pl.BlockSpec((NB, 1024), lambda t, *_: (t, 0)),
            full((2, PIV, 1024)),
            full((2, PIV, 1024)),
            full((2, 32, 1536)),
        ],
        scratch_shapes=[pltpu.VMEM((2, PIV, PIV), jnp.bfloat16)] * 2,
    )
    return pl.pallas_call(
        panel_kernel,
        grid_spec=grid_spec,
        out_shape=(
            jax.ShapeDtypeStruct((PIV, 1024), F32),
            jax.ShapeDtypeStruct((2, PIV, 1024), jnp.bfloat16),
            jax.ShapeDtypeStruct((2, PIV, 1024), jnp.bfloat16),
            jax.ShapeDtypeStruct((2, 32, 1536), F32),
        ),
        compiler_params=pltpu.CompilerParams(vmem_limit_bytes=56 << 20),
        cost_estimate=pl.CostEstimate(flops=10**10, bytes_accessed=1 << 25, transcendentals=0),
        name="panel_front",
    )(*maps, parent, rows, cols, inv, inv_part, *pieces)


def finish_kernel(info, rowi, rowv, colj, colv, parent, rows, inv, front, prows, pinv, *rest):
    (high, low), blocks, out = rest[:2], rest[2:18], rest[18]
    inv_h, inv_l, par_h, par_l = rest[19:]
    t = pl.program_id(0)

    @pl.when(t == 0)
    def _():
        for k in range(2):
            inv_h[k], inv_l[k] = split(inv[k])
        inv_h[2], inv_l[2] = split(pinv[...])
        for u in range(4):
            span = slice(u * NB, (u + 1) * NB)
            par_h[:, span], par_l[:, span] = split(
                dot3((inv_h[2], inv_l[2]), split(front[0, :, span]))
            )

    total = parent[...] + update_blocks(t, info, rowi, rowv, colj, colv, blocks)
    for m in range(2):
        k = info[0] if m == 0 else 1 - info[0]
        block = split(column_block(rows, k, rowi[m, t]))
        solved = dot3((inv_h[k], inv_l[k]), block)
        solved = jnp.where(rowv[m, t] > 0, solved, 0.0)
        total = total - dot3(split(solved.T), (high[m], low[m]))
    block = split(prows[0])
    solved = dot3((inv_h[2], inv_l[2]), block).T
    total = total - dot3(split(solved), (par_h[...], par_l[...]))
    in_pivots = (info[2] == 0) & (t < 2)
    wide = lax.broadcasted_iota(jnp.int32, total.shape, 0)
    total = jnp.where(in_pivots & (wide >= 0), 0.0, total)
    row_ids = t * NB + lax.broadcasted_iota(jnp.int32, solved.shape, 0)
    col_ids = lax.broadcasted_iota(jnp.int32, solved.shape, 1)
    factor = jnp.where(in_pivots & (col_ids > row_ids), 0.0, solved)
    lead = jnp.where((info[3] == 0) & (col_ids >= 0), factor, total[:, :PIV])
    out[:, :PIV] = lead
    out[:, PIV:] = total[:, PIV:]


def finish(maps, parent, rows, inv, front_cols, front_rows, front_inv, high, low, pieces):
    whole = pl.BlockSpec(memory_space=pltpu.VMEM)
    grid_spec = pltpu.PrefetchScalarGridSpec(
        num_scalar_prefetch=5,
        grid=(8,),
        in_specs=[
            pl.BlockSpec((NB, 1024), lambda t, *_: (t, 0)),
            whole,
            whole,
            pl.BlockSpec((1, PIV, 1024), lambda t, info, *_: (info[1], 0, 0)),
            pl.BlockSpec((1, PIV, NB), lambda t, *_: (t // 4, 0, t % 4)),
            whole,
            whole,
            whole,
            *block_specs(),
        ],
        out_specs=pl.BlockSpec((NB, 1024), lambda t, *_: (t, 0)),
        scratch_shapes=[
            *[pltpu.VMEM((3, PIV, PIV), jnp.bfloat16)] * 2,
            *[pltpu.VMEM((PIV, 1024), jnp.bfloat16)] * 2,
        ],
    )
    return pl.pallas_call(
        finish_kernel,
        grid_spec=grid_spec,
        out_shape=jax.ShapeDtypeStruct((2048, 1024), F32),
        compiler_params=pltpu.CompilerParams(vmem_limit_bytes=56 << 20),
        cost_estimate=pl.CostEstimate(flops=10**10, bytes_accessed=1 << 25, transcendentals=0),
        name="finish",
    )(*maps, parent, rows, inv, front_cols, front_rows, front_inv, high, low, *pieces)


def inverse_map(targets, first, places):
    blocks = first + jnp.arange(6, dtype=jnp.int32)
    usable = blocks >= PIV // NB
    wanted = jnp.clip(blocks - PIV // NB, 0, targets.shape[0] - 1)
    known = jnp.arange(targets.shape[0], dtype=jnp.int32)
    target = jnp.sum(jnp.where(known[None, :] == wanted[:, None], targets[None, :], 0), axis=1)
    hit = usable[:, None] & (target[:, None] == places[None, :])
    index = jnp.sum(jnp.where(hit, jnp.arange(6, dtype=jnp.int32)[:, None], 0), axis=0)
    return index.astype(jnp.int32), jnp.any(hit, axis=0).astype(jnp.int32)


def local(children, parent, relay_map):
    r = lax.axis_index("row")
    c = lax.axis_index("col")
    parity = r % 2
    g, h = c // 2, c % 2

    row_places = r * 8 + jnp.arange(8, dtype=jnp.int32)
    col_places = c * 4 + jnp.arange(4, dtype=jnp.int32)
    own_map = jnp.where(parity == 0, relay_map[0], relay_map[1])
    other_map = jnp.where(parity == 0, relay_map[1], relay_map[0])
    own_r = inverse_map(own_map, r * 6, row_places)
    other_r = inverse_map(other_map, r * 6, row_places)
    own_c = inverse_map(own_map, g * 6, col_places)
    other_c = inverse_map(other_map, g * 6, col_places)
    rowi, rowv = (jnp.stack(pair) for pair in zip(own_r, other_r))
    colj, colv = (jnp.stack(pair) for pair in zip(own_c, other_c))
    info = jnp.stack([parity, h, r, c]).astype(jnp.int32)
    maps = (info, rowi, rowv, colj, colv)

    shape = jax.ShapeDtypeStruct
    cols, rows, inv, (early, kept) = share(
        2, children, (), EarlyMoves(), (shape((2, 1024, 768), F32), shape((1536, 768), F32)), 0
    )
    inv_part = lax.dynamic_slice_in_dim(inv, c * 32, 32, 1)
    pieces = [children] * 4 + [kept] * 4 + [early] * 4
    front, high, low, factors = panel_front(
        maps, parent, rows, cols, inv, inv_part, pieces + [early] * 4
    )
    front_cols, front_rows, front_inv, (late, mates) = share(
        1,
        front,
        (children, factors),
        LateMoves(),
        (shape((2, 512, 768), F32), shape((32, 1536), F32)),
        1,
    )
    parent_out = finish(
        maps,
        parent,
        rows,
        inv,
        front_cols[:, 0],
        front_rows[:, 0],
        front_inv[0],
        high,
        low,
        pieces + [late] * 4,
    )
    mine = lax.dynamic_index_in_dim(factors, parity, 0, keepdims=False)
    first = jnp.where(parity == 0, mine, mates)
    second = jnp.where(parity == 0, mates, mine)
    child_factor = jnp.concatenate([first, second], axis=1).T
    row_ids = r // 2 * 3072 + jnp.arange(3072, dtype=jnp.int32)
    col_ids = c * 32 + jnp.arange(32, dtype=jnp.int32)
    child_factor = jnp.where(row_ids[:, None] >= col_ids[None, :], child_factor, 0.0)
    return parent_out, child_factor


def solution(mesh):
    return jax.shard_map(
        local,
        mesh=mesh,
        in_specs=(P("row", "col"), P("row", "col"), P()),
        out_specs=(P("row", "col"), P("row", "col")),
        check_vma=False,
    )
```

time: 538 us -> 450 us (0.84)
  the two profiles are of different devices: /device:TPU:57 before, /device:TPU:117 now
where the time goes in v2:
time: 450 us; the launch traced here: 444 us
  Pallas kernels  435 us (97%)
  other arithmetic  6.34 us (1%)
    pallas_call x2, Pallas kernels, share(): pl.pallas_call(kernel, out_shape=out_shape, in_specs=[pl.BlockSpec(memory...  351 us
    pallas_call x1, Pallas kernels, finish(): pl.pallas_call(finish_kernel, grid_spec=grid_spec, out_shape=jax.ShapeDty...  62.4 us
    pallas_call x1, Pallas kernels, panel_front(): pl.pallas_call(panel_kernel, grid_spec=grid_spec, out_shape=(jax.ShapeDty...  22.5 us

profile of v2, /device:TPU:117, one launch (start us, length us, event | category | flops | bytes accessed | tf_op | source)
XLA Modules:
  0.0 444.3 jit_solution(11344824086972144767)
XLA Ops:
  0.7 0.7 pad_add_fusion.2.info
  1.4 0.8 fusion.6
  2.2 0.2 select_reduce_fusion.1
  2.4 0.2 fusion.3
  2.6 0.2 select_reduce_fusion.7
  2.8 0.6 pad_add_fusion.1.colj
  3.3 0.5 add_convert_fusion.1.colv
  3.9 0.1 fusion.2
  4.0 0.1 select_reduce_fusion.4
  4.1 0.6 pad_add_fusion.rowi
  4.7 0.6 add_convert_fusion.rowv
  5.2 186.3 %share_panels_2.1 = (f32[2,2,512,768]{3,2,1,0:T(8,128)}, f32[2,2,512,768]{3,2,1,0:T(8,128)}, f32[2,2,8,32,512]{4,3,2,1,0:T(8,128)}, f32[2,1024,768]{2,1,0:T(8,128)}, f32[1536,768]{1,0:T(8,128)}) custom-call(f32[3072,768]{1,0:T(8,128)} %rest_5_.1), custom_call_target="tpu_custom_call" | custom-call | flops 10000000000 | bytes 33554432 | tf_op jit(solution)/shard_map/share_panels_2/pallas_call | solution.py:470
  191.6 1.6 constant_dynamic-slice_fusion.inv_part
  193.1 22.5 %panel_front.1 = (f32[512,1024]{1,0:T(8,128)}, bf16[2,512,1024]{2,1,0:T(8,128)(2,1)}, bf16[2,512,1024]{2,1,0:T(8,128)(2,1)}, f32[2,32,1536]{2,1,0:T(8,128)}) custom-call(s32[4]{0:T(128)} %pad_add_fusion.2.info, s32[2,8]{1,0:T(2,128)} %pad_add_fusion.rowi, s32[2,8]{1,0:T(2,128)} %add_convert_fusion.rowv, s32[2,4]{1,0:T(2,128)} %pad_add_fusion.1.colj, ...), custom_call_target="tpu_custom_call" | custom-call | flops 10000000000 | bytes 33554432 | tf_op jit(solution)/shard_map/panel_front/pallas_call | solution.py:600
  215.6 0.0 copy-start
  215.6 164.2 %share_panels_1.1 = (f32[2,1,512,1024]{3,2,1,0:T(8,128)}, f32[2,1,512,1024]{3,2,1,0:T(8,128)}, f32[1,2,8,32,512]{4,3,2,1,0:T(8,128)}, f32[2,512,768]{2,1,0:T(8,128)}, f32[32,1536]{1,0:T(8,128)}) custom-call(f32[512,1024]{1,0:T(8,128)} %get-tuple-element.21.refs_0_, f32[3072,768]{1,0:T(8,128)} %rest_5_.1, f32[2,32,1536]{2,1,0:T(8,128)} %get-tuple-element.22.refs_2_), custom_call_target="tpu_custom_call" | custom-call | flops 10000000000 | bytes 33554432 | tf_op jit(solution)/shard_map/share_panels_1/pallas_call | solution.py:470
  379.9 0.0 copy-done
  379.9 1.0 bitcast_select_fusion.1
  380.9 0.8 fusion
  381.7 62.4 %finish.1 = f32[2048,1024]{1,0:T(8,128)} custom-call(s32[4]{0:T(128)} %pad_add_fusion.2.info, s32[2,8]{1,0:T(2,128)} %pad_add_fusion.rowi, s32[2,8]{1,0:T(2,128)} %add_convert_fusion.rowv, s32[2,4]{1,0:T(2,128)} %pad_add_fusion.1.colj, s32[2,4]{1,0:T(2,128)} %add_convert_fusion.1.colv, f32[2048,1024]{1,0:T(8,128)} %parent.3, ...), custom_call_target="tpu_custom_call" | custom-call | flops 10000000000 | bytes 33554432 | tf_op jit(solution)/shard_map/finish/pallas_call | solution.py:674
  (7 shorter events, 0.0 us)
Async XLA Ops:
  215.6 164.3 %copy-start = (f32[2,32,1536]{2,1,0:T(8,128)S(1)}, f32[2,32,1536]{2,1,0:T(8,128)}, u32[]{:S(2)}) copy-start(f32[2,32,1536]{2,1,0:T(8,128)} %get-tuple-element.22.refs_2_) | copy-start | bytes 1179652

commit v3 on v2

v3 whole, which is shorter than its diff:
```python
import jax
import jax.numpy as jnp
from jax import lax
from jax.experimental import pallas as pl
from jax.experimental.pallas import tpu as pltpu
from jax.sharding import PartitionSpec as P

NB = 256
PIV = 512
HI = lax.Precision.HIGHEST
MESH = pl.DeviceIdType.MESH
F32 = jnp.float32


def nt(a, b):
    return lax.dot_general(a, b, (((1,), (1,)), ((), ())), precision=HI, preferred_element_type=jnp.float32)

def nn(a, b):
    return lax.dot_general(a, b, (((1,), (0,)), ((), ())), precision=HI, preferred_element_type=jnp.float32)

def diag_inverse(work, s):
    tiles = [work[pl.ds(s + 8 * t, 8), pl.ds(s, 128)] for t in range(16)]
    rows8 = lax.broadcasted_iota(jnp.int32, (8, 128), 0)
    lanes = lax.broadcasted_iota(jnp.int32, (8, 128), 1)
    unit = [jnp.where(rows8 + 8 * t == lanes, 1.0, 0.0) for t in range(16)]
    scales = [jnp.zeros((8, 1), jnp.float32) for t in range(16)]
    for j in range(128):
        tj, i = j // 8, j % 8
        pivot = tiles[tj][i:i + 1, j:j + 1]
        inv = 1.0 / pivot
        row = tiles[tj][i:i + 1, :] * inv
        mrow = unit[tj][i:i + 1, :] * inv
        for t in range(tj, 16):
            col = tiles[t][:, j:j + 1]
            if t == tj:
                col = jnp.where(rows8[:, :1] > i, col, 0.0)
            tiles[t] = tiles[t] - col * row
            unit[t] = unit[t] - col * mrow
    out = []
    for t in range(16):
        d = jnp.sum(jnp.where(rows8 + 8 * t == lanes, tiles[t], 0.0), axis=1, keepdims=True)
        out.append(unit[t] * lax.rsqrt(d))
    return jnp.concatenate(out, axis=0)

def start_factor(low, inv):
    inv[...] = jnp.zeros_like(inv)
    low[...] = jnp.zeros_like(low)


def factor_step(b, work, low, inv):
    s = pl.multiple_of(b * 128, 128)
    span = pl.ds(s, 128)
    d = diag_inverse(work, s)
    ids = lax.broadcasted_iota(jnp.int32, (PIV, 128), 0)
    beneath = jnp.where(ids >= s + 128, nt(work[:, span], d), 0.0)
    left = nn(low[span, :], inv[...])
    inv[span, :] = -nn(d, left)
    inv[span, span] = d
    low[:, span] = beneath
    work[...] = work[...] - nt(beneath, beneath)


def send(src, dst, send_sem, recv_sem, **device):
    return pltpu.make_async_remote_copy(
        src_ref=src,
        dst_ref=dst,
        send_sem=send_sem,
        recv_sem=recv_sem,
        device_id=device,
        device_id_type=MESH,
    )


def share_kernel(members, moves, *refs):
    src = refs[0]
    refs = refs[1:]
    extra_in, refs = refs[: moves.inputs], refs[moves.inputs :]
    (cols, rows, inv), refs = refs[:3], refs[3:]
    extra_out, refs = refs[: moves.outputs], refs[moves.outputs :]
    work, low, made, diag_sem, here, *sems = refs
    (col_put, col_got, col_out, col_in, col_swap, col_over) = sems[:6]
    (row_put, row_got, row_swap, row_out, row_in, row_over) = sems[6:12]
    (inv_put, inv_got, inv_down, inv_down_got, inv_out, inv_in, inv_over) = sems[12:19]
    move_sems = sems[19:]

    r = lax.axis_index("row")
    c = lax.axis_index("col")
    g, h = c // 2, c % 2
    other = c + 1 - 2 * h
    mate = r + 1 - 2 * (r % 2)
    strip, quarter = PIV // 8, PIV // 4
    plane, level = r // 4, r % 4
    ring, side = c // 4, c // 2 % 2
    parity = r % 2
    giver = r < members
    root = giver & (c == 0)
    home = giver & (g == r)

    barrier = pltpu.get_barrier_semaphore()

    def greet(row, col):
        pl.semaphore_signal(barrier, 1, device_id={"row": row, "col": col}, device_id_type=MESH)

    for d in range(1, 4):
        greet(plane * 4 + (level + d) % 4, c)
    greet((1 - plane) * 4 + level, c)
    for d in range(1, 8):
        greet(r, (g + d) % 8 * 2 + h)
    greet(r, other)
    for k in range(members):
        pl.when(r != k)(lambda k=k: greet(k, c))
    if members == 2:
        pl.when(c != 0)(lambda: greet(r, 0))
        greet(mate, 0)
        count = 12 + jnp.where(giver, 7, 0) + jnp.where(c == 0, 31, 0)
    else:
        pl.when(jnp.logical_not(home))(lambda: greet(0, 2 * r + h))
        pl.when(giver & (c != 0))(lambda: greet(0, 0))
        count = 12 + jnp.where(giver, 15, 0) - jnp.where(home, 1, 0) + jnp.where(root, 15, 0)
    pl.semaphore_wait(barrier, count)

    def part(index):
        return pl.ds(pl.multiple_of(index * strip, strip), strip)

    def slot(k, index):
        return cols.at[h, k, part(index), :]

    def row_slot(k, index):
        return rows.at[k, h, index] if members == 2 else rows.at[h, k, part(index), :]

    def col_scatter(k, d):
        dest = (r + d) % 8
        return send(
            src.at[part(dest), :],
            slot(k, dest),
            col_put.at[d],
            col_got.at[k],
            row=dest,
            col=c,
        )

    def row_piece(target, dest):
        start = target % 2 * 1536 + (dest % 2 * 8 + dest // 2) * 96
        return src.at[pl.ds(pl.multiple_of(start, 32), 96), pl.ds(0, PIV)]

    def row_scatter(d, to_mate=False):
        if members == 2:
            dest = (c + d) % 16
            target = mate if to_mate else r
            return send(
                row_piece(target, dest),
                rows.at[parity, dest % 2, dest // 2],
                row_put.at[1 if to_mate else 0, d],
                row_got.at[parity],
                row=target,
                col=dest,
            )
        return send(
            src.at[part(d), :],
            row_slot(0, d),
            row_put.at[0, d],
            row_got.at[0],
            row=g,
            col=2 * d + h,
        )

    def row_taken(k):
        return send(
            row_slot(k, g), row_slot(k, g), row_put.at[0, 0], row_got.at[k], row=r, col=other
        )

    def inv_scatter(k, d):
        dest = (c + d) % 16
        at = (dest % 2 * 8 + dest // 2) * 32
        return send(
            made.at[pl.ds(pl.multiple_of(at, 32), 32), :],
            inv.at[k, dest % 2, dest // 2],
            inv_put.at[d],
            inv_got.at[k],
            row=r,
            col=dest,
        )

    local_diag = pltpu.make_async_copy(src.at[pl.ds(0, PIV), pl.ds(0, PIV)], work, diag_sem.at[0])
    local_col = pltpu.make_async_copy(src.at[part(r), :], slot(r, r), here.at[1])
    local_row = pltpu.make_async_copy(
        row_piece(r, 0) if members == 2 else src.at[part(g), :],
        row_slot(parity if members == 2 else 0, g),
        here.at[0],
    )
    local_inv = pltpu.make_async_copy(made.at[pl.ds(0, 32), :], inv.at[r, 0, 0], here.at[2])

    @pl.when(root)
    def _():
        local_diag.start()

    @pl.when(giver)
    def _():
        local_col.start()

        @pl.loop(1, 8)
        def _(d):
            col_scatter(r, d).start()

    if members == 2:

        @pl.when(c == 0)
        def _():
            local_row.start()

            @pl.loop(1, 16)
            def _(d):
                row_scatter(d).start()

            row_scatter(0, True).start()

            @pl.loop(1, 16)
            def _(d):
                row_scatter(d, True).start()

    else:

        @pl.when(giver)
        def _():
            @pl.loop(0, 8)
            def _(d):
                @pl.when(jnp.logical_not(home & (g == d)))
                def _():
                    row_scatter(d).start()

        @pl.when(home)
        def _():
            local_row.start()

    block_move, aside = moves.copies(extra_in, extra_out, move_sems, src, r, c, h, mate, other)

    def each_block(act):
        for index in range(6):
            pl.when(moves.sends(r, index))(lambda index=index: act(index))

    @pl.when(root)
    def _():
        local_diag.wait()
        start_factor(low, made)
        factor_step(0, work, low, made)

    def col_gather(d, arriving=False):
        peer = (level + d) % 4
        at = plane * 4 + (peer if arriving else level)
        strips = cols.at[h, :, part(at), :]
        return send(
            strips, strips, col_out.at[d], col_in.at[at % 4], row=plane * 4 + peer, col=c
        )

    def col_half(from_plane):
        rows_of = pl.ds(pl.multiple_of(from_plane * NB, NB), NB)
        half = cols.at[h, :, rows_of, :]
        return send(half, half, col_swap.at[0], col_swap.at[1], row=(1 - plane) * 4 + level, col=c)

    pair = c + 2 - 4 * side

    def row_pair(k, arriving=False):
        strips = row_slot(k, g + 1 - 2 * side if arriving else g)
        return send(strips, strips, row_swap.at[0, k], row_swap.at[1, k], row=r, col=pair)

    def row_gather(k, d, arriving=False):
        peer = (ring + d) % 4
        at = peer if arriving else ring
        if members == 2:
            strips = rows.at[k, h, pl.ds(2 * at, 2)]
        else:
            strips = rows.at[h, k, pl.ds(pl.multiple_of(at * 2 * strip, 2 * strip), 2 * strip), :]
        return send(
            strips,
            strips,
            row_out.at[k, d],
            row_in.at[k, at],
            row=r,
            col=peer * 4 + side * 2 + h,
        )

    row_order = (parity, 1 - parity) if members == 2 else (0,)

    def inv_column(k, d):
        return send(
            inv.at[k, h, g],
            inv.at[k, h, g],
            inv_down.at[d],
            inv_down_got.at[k],
            row=(r + d) % 8,
            col=c,
        )

    def inv_gather(d, arriving=False):
        peer = (g + d) % 8
        at = peer if arriving else g
        part_of = inv.at[:, h, at]
        return send(part_of, part_of, inv_out.at[d], inv_in.at[at], row=r, col=peer * 2 + h)

    def cross(buffer, sems):
        return send(buffer, buffer, sems.at[0], sems.at[1], row=r, col=other)

    def row_cross(half):
        return cross(rows.at[:, half] if members == 2 else rows.at[half], row_over)

    for k in range(members):

        @pl.when(r == k)
        def _():
            local_col.wait()

        @pl.when(r != k)
        def _():
            col_scatter(k, 1).wait_recv()

    @pl.loop(1, 4)
    def _(d):
        col_gather(d).start()

    for turn, k in enumerate(row_order):
        holds = (c == 0) & (turn == 0) if members == 2 else home

        @pl.when(holds)
        def _():
            local_row.wait()

        @pl.when(jnp.logical_not(holds))
        def _():
            row_taken(k).wait_recv()

        row_pair(k).start()

    each_block(lambda index: block_move(index).start())
    aside().start()

    @pl.when(root)
    def _():
        @pl.loop(1, 3)
        def _(b):
            factor_step(b, work, low, made)

    for k in row_order:
        row_pair(k, True).wait_recv()

        @pl.loop(1, 4)
        def _(d):
            row_gather(k, d).start()

    @pl.loop(1, 4)
    def _(d):
        col_gather(d, True).wait_recv()

    col_half(plane).start()

    @pl.when(root)
    def _():
        factor_step(3, work, low, made)

        local_inv.start()

        @pl.loop(1, 16)
        def _(d):
            inv_scatter(r, d).start()

        local_inv.wait()

    for k in range(members):

        @pl.when((r == k) & (c != 0))
        def _():
            inv_scatter(k, 1).wait_recv()

        @pl.when(r == k)
        def _():
            @pl.loop(1, 8)
            def _(d):
                inv_column(k, d).start()

    for k in range(members):

        @pl.when(r != k)
        def _():
            inv_column(k, 1).wait_recv()

    @pl.loop(1, 8)
    def _(d):
        inv_gather(d).start()

    col_half(1 - plane).wait_recv()
    if members == 2:
        cross(cols.at[h], col_over).start()

    for k in row_order:

        @pl.loop(1, 4)
        def _(d):
            row_gather(k, d, True).wait_recv()

    row_cross(h).start()

    @pl.loop(1, 8)
    def _(d):
        inv_gather(d, True).wait_recv()

    cross(inv.at[:, h], inv_over).start()

    def pass_on(index):
        block_move(index).wait_recv()
        block_move(index, True).start()

    each_block(pass_on)

    if members == 2:
        cross(cols.at[1 - h], col_over).wait_recv()
        cross(cols.at[h], col_over).wait_send()
    col_half(plane).wait_send()
    row_cross(1 - h).wait_recv()
    row_cross(h).wait_send()
    cross(inv.at[:, 1 - h], inv_over).wait_recv()
    cross(inv.at[:, h], inv_over).wait_send()

    def settle(index):
        block_move(index).wait_send()
        block_move(index, True).wait()

    each_block(settle)
    aside().wait()

    @pl.loop(1, 4)
    def _(d):
        col_gather(d).wait_send()

    @pl.loop(1, 8)
    def _(d):
        inv_gather(d).wait_send()

    for k in row_order:
        row_pair(k).wait_send()

        @pl.loop(1, 4)
        def _(d):
            row_gather(k, d).wait_send()

    for k in range(members):

        @pl.when(r == k)
        def _():
            @pl.loop(1, 8)
            def _(d):
                col_scatter(k, d).wait_send()
                inv_column(k, d).wait_send()

        @pl.when((r == k) & (c == 0))
        def _():
            @pl.loop(1, 16)
            def _(d):
                inv_scatter(k, d).wait_send()

    if members == 2:

        @pl.when(c == 0)
        def _():
            @pl.loop(1, 16)
            def _(d):
                row_scatter(d).wait_send()

            @pl.loop(0, 16)
            def _(d):
                row_scatter(d, True).wait_send()

    else:

        @pl.when(giver)
        def _():
            @pl.loop(0, 8)
            def _(d):
                @pl.when(jnp.logical_not(home & (g == d)))
                def _():
                    row_scatter(d).wait_send()


class Moves:
    def __init__(self, first):
        self.first = first
        self.inputs, self.outputs = (0, 2) if first else (3, 2)

    def sends(self, r, index):
        early = (r < 2) & (index >= 2) if index < 4 else r >= 0
        return early if self.first else jnp.logical_not(early)

    def copies(self, ins, outs, sems, src, r, c, h, mate, other):
        (got, extra), (put_sem, got_sem, over_put, over_got) = outs, sems
        children = src if self.first else ins[0]

        def block(index, relay=False):
            place = got.at[h, pl.ds(index * NB, NB), :]
            if relay:
                return send(place, place, over_put.at[index], over_got.at[index], row=r, col=other)
            rows = pl.ds(pl.multiple_of((1 - r % 2) * 1536 + index * NB, NB), NB)
            return send(
                children.at[rows, :], place, put_sem.at[index], got_sem.at[index], row=mate, col=c
            )

        def aside():
            if self.first:
                rows = pl.ds(pl.multiple_of(r % 2 * 1536, NB), 1536)
                return send(
                    src.at[rows, :], extra, put_sem.at[6], got_sem.at[6], row=r, col=other
                )
            return send(
                ins[1].at[1 - r % 2], extra, put_sem.at[6], got_sem.at[6], row=mate, col=c
            )

        return block, aside


def share(members, source, extras, extra_shapes, collective_id):
    moves = Moves(members == 2)
    width = source.shape[1]
    dma = pltpu.SemaphoreType.DMA
    shape = jax.ShapeDtypeStruct
    row_shape = (2, 2, 8, 96, PIV) if members == 2 else (2, 1, PIV, width)
    out_shape = (
        shape((2, members, PIV, width), F32),
        shape(row_shape, F32),
        shape((members, 2, 8, 32, PIV), F32),
        *extra_shapes,
    )
    scratch = [
        *[pltpu.VMEM((PIV, PIV), F32)] * 3,
        dma((1,)),
        dma((3,)),
        dma((8,)),
        dma((members,)),
        dma((4,)),
        dma((4,)),
        dma((2,)),
        dma((2,)),
        dma((2, 16)),
        dma((members,)),
        dma((2, members)),
        dma((members, 4)),
        dma((members, 4)),
        dma((2,)),
        dma((16,)),
        dma((members,)),
        dma((8,)),
        dma((members,)),
        dma((8,)),
        dma((8,)),
        dma((2,)),
        dma((7,)),
        dma((7,)),
        dma((6,)),
        dma((6,)),
    ]

    def kernel(*refs):
        share_kernel(members, moves, *refs)

    cols, rows, inv, *extra = pl.pallas_call(
        kernel,
        out_shape=out_shape,
        in_specs=[pl.BlockSpec(memory_space=pl.ANY)] * (1 + len(extras)),
        out_specs=[pl.BlockSpec(memory_space=pl.ANY)] * len(out_shape),
        scratch_shapes=scratch,
        input_output_aliases={} if members == 2 else {3: 3},
        compiler_params=pltpu.CompilerParams(
            collective_id=collective_id, has_side_effects=True, vmem_limit_bytes=56 << 20
        ),
        cost_estimate=pl.CostEstimate(flops=10**10, bytes_accessed=1 << 25, transcendentals=0),
        name="share_panels_%d" % members,
    )(source, *extras)
    if members == 2:
        rows = rows.reshape(2, 1536, PIV)
    return cols, rows, inv.reshape(members, PIV, PIV), extra


def split(value):
    high = value.astype(jnp.bfloat16)
    return high, (value - high.astype(F32)).astype(jnp.bfloat16)


def left_terms(value):
    high, low = split(value)
    return jnp.concatenate([high, high, low], axis=1)


def right_terms(value):
    high, low = split(value)
    return jnp.concatenate([high, low, high], axis=0)


def dot(left, right):
    return jnp.dot(left, right, preferred_element_type=F32)


def column_block(panels, k, block):
    at = pl.multiple_of(block % 3 * NB, NB)
    return panels[block // 3, k, :, pl.ds(at, NB)]


def update_blocks(t, info, rowi, rowv, colj, colv, blocks):
    total = None
    for m in range(2):
        adds = []
        for u in range(4):
            first, second = blocks[m * 4 + u], blocks[8 + u]
            use = (rowv[m, t] > 0) & (colv[m, u] > 0)
            if m == 0:
                block = jnp.where(colj[m, u] // 3 == info[1], second[...], first[...])
            else:
                block = first[0]
            adds.append(jnp.where(use, block, 0.0))
        sum_m = jnp.concatenate(adds, axis=1)
        total = sum_m if total is None else total + sum_m
    return total


def block_specs():
    def own(u, place):
        def index(t, info, rowi, rowv, colj, colv):
            here = colj[0, u] // 3 == info[1]
            want = here if place == 0 else jnp.logical_not(here)
            row = rowi[0, t] + (info[0] * 6 if place == 0 else 0)
            return (jnp.where(want, row, 0), jnp.where(want, colj[0, u] % 3, 0))

        return pl.BlockSpec((NB, NB), index)

    def mates(u):
        def index(t, info, rowi, rowv, colj, colv):
            return (colj[1, u] // 3, rowi[1, t], colj[1, u] % 3)

        return pl.BlockSpec((1, NB, NB), index)

    return [
        *[own(u, 1) for u in range(4)],
        *[mates(u) for u in range(4)],
        *[own(u, 0) for u in range(4)],
    ]


def row_terms(value):
    high, low = split(value)
    return jnp.concatenate([high, low, high], axis=1)


def dot_t(left, right):
    return lax.dot_general(left, right, (((1,), (1,)), ((), ())), preferred_element_type=F32)


def panel_kernel(info, rowi, rowv, colj, colv, parent, rows, cols, inv, inv_part, *rest):
    blocks, (front, solved_cols, factors), (inv_terms,) = rest[:12], rest[12:15], rest[15:]
    t = pl.program_id(0)

    @pl.when(t == 0)
    def _():
        for k in range(2):
            inv_terms[k] = left_terms(inv[k])
        for m in range(2):
            k = info[0] if m == 0 else 1 - info[0]
            for u in range(4):
                block = right_terms(column_block(cols, k, colj[m, u]))
                solved = dot(inv_terms[k], block)
                solved = jnp.where(colv[m, u] > 0, solved, 0.0)
                solved_cols[m, :, u * NB : (u + 1) * NB] = right_terms(solved)
        for k in range(2):
            factors[k] = dot_t(left_terms(inv_part[k]), row_terms(rows[k]))

    total = parent[...] + update_blocks(t, info, rowi, rowv, colj, colv, blocks)
    for m in range(2):
        k = info[0] if m == 0 else 1 - info[0]
        block = rows[k, pl.ds(pl.multiple_of(rowi[m, t] * NB, NB), NB), :]
        solved = dot_t(left_terms(block), row_terms(inv[k]))
        solved = jnp.where(rowv[m, t] > 0, solved, 0.0)
        total = total - dot(left_terms(solved), solved_cols[m])
    front[...] = total


def panel_front(maps, parent, rows, cols, inv, inv_part, pieces):
    whole = pl.BlockSpec(memory_space=pltpu.VMEM)
    full = lambda shape: pl.BlockSpec(shape, lambda t, *_: (0,) * len(shape))
    grid_spec = pltpu.PrefetchScalarGridSpec(
        num_scalar_prefetch=5,
        grid=(2,),
        in_specs=[
            pl.BlockSpec((NB, 1024), lambda t, *_: (t, 0)),
            whole,
            whole,
            whole,
            whole,
            *block_specs(),
        ],
        out_specs=[
            pl.BlockSpec((NB, 1024), lambda t, *_: (t, 0)),
            full((2, 3 * PIV, 1024)),
            full((2, 32, 1536)),
        ],
        scratch_shapes=[pltpu.VMEM((2, PIV, 3 * PIV), jnp.bfloat16)],
    )
    return pl.pallas_call(
        panel_kernel,
        grid_spec=grid_spec,
        out_shape=(
            jax.ShapeDtypeStruct((PIV, 1024), F32),
            jax.ShapeDtypeStruct((2, 3 * PIV, 1024), jnp.bfloat16),
            jax.ShapeDtypeStruct((2, 32, 1536), F32),
        ),
        compiler_params=pltpu.CompilerParams(vmem_limit_bytes=60 << 20),
        cost_estimate=pl.CostEstimate(flops=10**10, bytes_accessed=1 << 25, transcendentals=0),
        name="panel_front",
    )(*maps, parent, rows, cols, inv, inv_part, *pieces)


def finish_kernel(info, rowi, rowv, colj, colv, parent, rows, inv, fcols, frows, finv, *rest):
    solved_cols, blocks, out = rest[0], rest[1:13], rest[13]
    inv_terms, par_cols, high, low, par_rows = rest[14:]
    t = pl.program_id(0)

    @pl.when(t == 0)
    def _():
        for m in range(2):
            k = info[0] if m == 0 else 1 - info[0]
            inv_terms[...] = row_terms(inv[k])
            for part in range(3):
                span = slice(part * PIV, (part + 1) * PIV)
                block = left_terms(rows[k, span, :])
                high[m, span, :], low[m, span, :] = split(dot_t(block, inv_terms[...]))
        inv_terms[...] = left_terms(finv[...])
        for u in range(4):
            span = slice(u * NB, (u + 1) * NB)
            par_cols[:, span] = right_terms(dot(inv_terms[...], right_terms(fcols[0, :, span])))
            for half in range(2):
                solved = dot(inv_terms[...], right_terms(frows[half, :, span])).T
                par_rows[half * 1024 + u * NB : half * 1024 + (u + 1) * NB, :] = solved

    solved = par_rows[pl.ds(pl.multiple_of(t * NB, NB), NB), :]
    total = parent[...] + update_blocks(t, info, rowi, rowv, colj, colv, blocks)
    out[...] = total - dot(left_terms(solved), par_cols[...])
    for m in range(2):

        @pl.when(rowv[m, t] > 0)
        def _():
            span = pl.ds(pl.multiple_of(rowi[m, t] * NB, NB), NB)
            left = jnp.concatenate([high[m, span, :], high[m, span, :], low[m, span, :]], axis=1)
            out[...] -= dot(left, solved_cols[m])

    @pl.when((info[2] == 0) & (t < 2))
    def _():
        out[...] = jnp.zeros_like(out)

    @pl.when(info[3] == 0)
    def _():
        row_ids = t * NB + lax.broadcasted_iota(jnp.int32, solved.shape, 0)
        col_ids = lax.broadcasted_iota(jnp.int32, solved.shape, 1)
        above = (info[2] == 0) & (col_ids > row_ids)
        out[:, :PIV] = jnp.where(above, 0.0, solved)


def finish(maps, parent, rows, inv, front_cols, front_rows, front_inv, solved_cols, pieces):
    whole = pl.BlockSpec(memory_space=pltpu.VMEM)
    grid_spec = pltpu.PrefetchScalarGridSpec(
        num_scalar_prefetch=5,
        grid=(8,),
        in_specs=[
            pl.BlockSpec((NB, 1024), lambda t, *_: (t, 0)),
            whole,
            whole,
            pl.BlockSpec((1, PIV, 1024), lambda t, info, *_: (info[1], 0, 0)),
            whole,
            whole,
            whole,
            *block_specs(),
        ],
        out_specs=pl.BlockSpec((NB, 1024), lambda t, *_: (t, 0)),
        scratch_shapes=[
            pltpu.VMEM((PIV, 3 * PIV), jnp.bfloat16),
            pltpu.VMEM((3 * PIV, 1024), jnp.bfloat16),
            pltpu.VMEM((2, 1536, PIV), jnp.bfloat16),
            pltpu.VMEM((2, 1536, PIV), jnp.bfloat16),
            pltpu.VMEM((2048, PIV), F32),
        ],
    )
    return pl.pallas_call(
        finish_kernel,
        grid_spec=grid_spec,
        out_shape=jax.ShapeDtypeStruct((2048, 1024), F32),
        compiler_params=pltpu.CompilerParams(vmem_limit_bytes=60 << 20),
        cost_estimate=pl.CostEstimate(flops=10**10, bytes_accessed=1 << 25, transcendentals=0),
        name="finish",
    )(*maps, parent, rows, inv, front_cols, front_rows, front_inv, solved_cols, *pieces)


def inverse_map(targets, first, places):
    blocks = first + jnp.arange(6, dtype=jnp.int32)
    usable = blocks >= PIV // NB
    wanted = jnp.clip(blocks - PIV // NB, 0, targets.shape[0] - 1)
    known = jnp.arange(targets.shape[0], dtype=jnp.int32)
    target = jnp.sum(jnp.where(known[None, :] == wanted[:, None], targets[None, :], 0), axis=1)
    hit = usable[:, None] & (target[:, None] == places[None, :])
    index = jnp.sum(jnp.where(hit, jnp.arange(6, dtype=jnp.int32)[:, None], 0), axis=0)
    return index.astype(jnp.int32), jnp.any(hit, axis=0).astype(jnp.int32)


def local(children, parent, relay_map):
    r = lax.axis_index("row")
    c = lax.axis_index("col")
    parity = r % 2
    g, h = c // 2, c % 2

    row_places = r * 8 + jnp.arange(8, dtype=jnp.int32)
    col_places = c * 4 + jnp.arange(4, dtype=jnp.int32)
    own_map = jnp.where(parity == 0, relay_map[0], relay_map[1])
    other_map = jnp.where(parity == 0, relay_map[1], relay_map[0])
    own_r = inverse_map(own_map, r * 6, row_places)
    other_r = inverse_map(other_map, r * 6, row_places)
    own_c = inverse_map(own_map, g * 6, col_places)
    other_c = inverse_map(other_map, g * 6, col_places)
    rowi, rowv = (jnp.stack(pair) for pair in zip(own_r, other_r))
    colj, colv = (jnp.stack(pair) for pair in zip(own_c, other_c))
    info = jnp.stack([parity, h, r, c]).astype(jnp.int32)
    maps = (info, rowi, rowv, colj, colv)

    shape = jax.ShapeDtypeStruct
    cols, rows, inv, (got, kept) = share(
        2, children, (), (shape((2, 1536, 768), F32), shape((1536, 768), F32)), 0
    )
    inv_part = lax.dynamic_slice_in_dim(inv, c * 32, 32, 1)
    pieces = lambda got: [kept] * 4 + [got] * 4 + [children] * 4
    front, solved_cols, factors = panel_front(
        maps, parent, rows, cols, inv, inv_part, pieces(got)
    )
    front_cols, front_rows, front_inv, (got, mates) = share(
        1,
        front,
        (children, factors, got),
        (shape((2, 1536, 768), F32), shape((32, 1536), F32)),
        1,
    )
    parent_out = finish(
        maps,
        parent,
        rows,
        inv,
        front_cols[:, 0],
        front_rows[:, 0],
        front_inv[0],
        solved_cols,
        pieces(got),
    )
    mine = lax.dynamic_index_in_dim(factors, parity, 0, keepdims=False)
    first = jnp.where(parity == 0, mine, mates)
    second = jnp.where(parity == 0, mates, mine)
    child_factor = jnp.concatenate([first, second], axis=1).T
    row_ids = r // 2 * 3072 + jnp.arange(3072, dtype=jnp.int32)
    col_ids = c * 32 + jnp.arange(32, dtype=jnp.int32)
    child_factor = jnp.where(row_ids[:, None] >= col_ids[None, :], child_factor, 0.0)
    return parent_out, child_factor


def solution(mesh):
    return jax.shard_map(
        local,
        mesh=mesh,
        in_specs=(P("row", "col"), P("row", "col"), P()),
        out_specs=(P("row", "col"), P("row", "col")),
        check_vma=False,
    )
```

time: 450 us -> 364 us (0.81)
  the two profiles are of different devices: /device:TPU:117 before, /device:TPU:57 now
where the time goes in v3:
time: 364 us; the launch traced here: 359 us
  Pallas kernels  350 us (96%)
  other arithmetic  6.34 us (2%)
    pallas_call x2, Pallas kernels, share(): pl.pallas_call(kernel, out_shape=out_shape, in_specs=[pl.BlockSpec(memory...  283 us
    pallas_call x1, Pallas kernels, finish(): pl.pallas_call(finish_kernel, grid_spec=grid_spec, out_shape=jax.ShapeDty...  43.8 us
    pallas_call x1, Pallas kernels, panel_front(): pl.pallas_call(panel_kernel, grid_spec=grid_spec, out_shape=(jax.ShapeDty...  23.2 us

profile of v3, /device:TPU:57, one launch (start us, length us, event | category | flops | bytes accessed | tf_op | source)
XLA Modules:
  0.0 358.7 jit_solution(4631530116003167270)
XLA Ops:
  0.7 0.8 fusion.6
  1.4 0.2 select_reduce_fusion.1
  1.7 0.2 fusion.3
  1.9 0.6 add_convert_fusion.1.colv
  2.4 0.2 select_reduce_fusion.7
  2.6 0.6 pad_add_fusion.1.colj
  3.2 0.1 fusion.2
  3.3 0.6 add_convert_fusion.rowv
  3.9 0.1 select_reduce_fusion.4
  4.0 0.6 pad_add_fusion.rowi
  4.6 0.6 pad_add_fusion.2.info
  5.2 143.5 %share_panels_2.1 = (f32[2,2,512,768]{3,2,1,0:T(8,128)}, f32[2,2,8,96,512]{4,3,2,1,0:T(8,128)}, f32[2,2,8,32,512]{4,3,2,1,0:T(8,128)}, f32[2,1536,768]{2,1,0:T(8,128)}, f32[1536,768]{1,0:T(8,128)}) custom-call(f32[3072,768]{1,0:T(8,128)} %rest_12_.1), custom_call_target="tpu_custom_call" | custom-call | flops 10000000000 | bytes 33554432 | tf_op jit(solution)/shard_map/share_panels_2/pallas_call | solution.py:561
  148.7 1.6 constant_dynamic-slice_fusion.inv_part
  150.3 23.2 %panel_front.1 = (f32[512,1024]{1,0:T(8,128)}, bf16[2,1536,1024]{2,1,0:T(8,128)(2,1)}, f32[2,32,1536]{2,1,0:T(8,128)}) custom-call(s32[4]{0:T(128)} %pad_add_fusion.2.info, s32[2,8]{1,0:T(2,128)} %pad_add_fusion.rowi, s32[2,8]{1,0:T(2,128)} %add_convert_fusion.rowv, s32[2,4]{1,0:T(2,128)} %pad_add_fusion.1.colj, s32[2,4]{1,0:T(2,128)} %add_convert_fusion.1.colv, ...), custom_call_target="tpu_custom_call" | custom-call | flops 10000000000 | bytes 33554432 | tf_op jit(solution)/shard_map/panel_front/pallas_call | solution.py:701
  173.5 0.0 copy-start
  173.5 139.3 %share_panels_1.1 = (f32[2,1,512,1024]{3,2,1,0:T(8,128)}, f32[2,1,512,1024]{3,2,1,0:T(8,128)}, f32[1,2,8,32,512]{4,3,2,1,0:T(8,128)}, f32[2,1536,768]{2,1,0:T(8,128)}, f32[32,1536]{1,0:T(8,128)}) custom-call(f32[512,1024]{1,0:T(8,128)} %get-tuple-element.20.refs_0_, f32[3072,768]{1,0:T(8,128)} %rest_12_.1, ...), custom_call_target="tpu_custom_call", output_to_operand_aliasing={{3}: (3, {})} | custom-call | flops 10000000000 | bytes 33554432 | tf_op jit(solution)/shard_map/share_panels_1/pallas_call | solution.py:561
  312.8 0.0 copy-done
  312.8 1.0 bitcast_select_fusion.1
  313.8 0.8 fusion
  314.7 43.8 %finish.1 = f32[2048,1024]{1,0:T(8,128)} custom-call(s32[4]{0:T(128)} %pad_add_fusion.2.info, s32[2,8]{1,0:T(2,128)} %pad_add_fusion.rowi, s32[2,8]{1,0:T(2,128)} %add_convert_fusion.rowv, s32[2,4]{1,0:T(2,128)} %pad_add_fusion.1.colj, s32[2,4]{1,0:T(2,128)} %add_convert_fusion.1.colv, f32[2048,1024]{1,0:T(8,128)} %parent.3, f32[2,1536,512]{2,1,0:T(8,128)} %bitcast.29, ...), custom_call_target="tpu_custom_call" | custom-call | flops 10000000000 | bytes 33554432 | tf_op jit(solution)/shard_map/finish/pallas_call | solution.py:784
  (7 shorter events, 0.0 us)
Async XLA Ops:
  173.5 139.3 %copy-start = (f32[2,32,1536]{2,1,0:T(8,128)S(1)}, f32[2,32,1536]{2,1,0:T(8,128)}, u32[]{:S(2)}) copy-start(f32[2,32,1536]{2,1,0:T(8,128)} %get-tuple-element.21.refs_2_) | copy-start | bytes 1179652
